TPU v7x, 32 devices: a whole 2x2x4 slice. The times are simulated.
32 devices in a mesh: groups: 2 (over y), seq: 16 (over z, x, core).
Axes of the slice: x: 2, y: 2, z: 4, core: 2. Of those that a mesh axis runs over, the one named last changes fastest.
Arguments:
- queries: bfloat16 [32768, 512], P(('groups', 'seq')), parts along dimension 0, may hold values from -8 to 8
- video_keys: bfloat16 [32768, 512], P(('groups', 'seq')), parts along dimension 0, may hold values from -8 to 8
- video_values: bfloat16 [32768, 512], P(('groups', 'seq')), parts along dimension 0, may hold values from -6 to 6
- text_keys: bfloat16 [512, 512], P(('groups', 'seq')), parts along dimension 0, may hold values from -6 to 6
- text_values: bfloat16 [512, 512], P(('groups', 'seq')), parts along dimension 0, may hold values from -6 to 6
- block_lists: int32 [4, 256, 9], P(None, ('groups', 'seq')), parts along dimension 1, may hold values from 0 to 127, as said below
- list_lengths: int32 [4, 256], P(None, ('groups', 'seq')), parts along dimension 1, may hold values from 1 to 9, as said below
Outputs:
- attended: bfloat16 [32768, 512], P(('groups', 'seq')), parts along dimension 0
There are 2 independent parts, one for each index of `groups`. A program takes and returns all parts, laid end to end along the dimension named above; each array names one. Nothing has to cross between parts.
Inputs may be any that keep to these rules, and one draw needn't show every extreme that they name: `block_lists`: the list of head h and query block a starts with a itself, followed by list_lengths[h, a] - 1 other distinct key blocks b with |b - a| <= 8; entries from position list_lengths[h, a] on equal a. `list_lengths`: some list is 9 long and some list is 1 long in every draw.
All inputs are finite; a program needn't handle non-finite values.
Results may differ from a plain program's by a relative error of at most 0.0055.
Values may be sent and summed in bfloat16 or wider, within the bound.
No kernel may reach another device: no remote copies, remote signals or barrier semaphores. Data moves between devices by JAX's collectives and lax.ppermute only.
A program may use at most 64 MiB of HBM per device.

v0:
```python
import functools
import math

import jax
import jax.numpy as jnp
from jax import lax
from jax.experimental import pallas as pl
from jax.experimental.pallas import tpu as pltpu
from jax.sharding import PartitionSpec as P

HEAD_DIM = 128
HEADS = 4
BLOCK = 128
REACH = 8
GROUP = 16
EXP2_SCALE = HEAD_DIM ** (-0.5) * math.log2(math.e)
NEVER = -1e30
NT = (((1,), (1,)), ((), ()))
VMEM_BYTES = 60 * 1024 * 1024
CODE = 64


def aligned(index):
    return pl.ds(pl.multiple_of(index * BLOCK, BLOCK), BLOCK)


def score_tile(keys, query_rows):
    return lax.dot_general(keys, query_rows, NT, preferred_element_type=jnp.float32)


def partial_attention(keys, query_rows, values_t):
    scores = score_tile(keys, query_rows)
    top = jnp.max(scores, axis=0, keepdims=True)
    weights = jnp.exp2((scores - top) * EXP2_SCALE)
    total = jnp.sum(weights, axis=0, keepdims=True)
    summed = jnp.dot(values_t, weights.astype(jnp.bfloat16), preferred_element_type=jnp.float32)
    return top, total, summed


def merge(unit, part, tops, totals, sums):
    top, total, summed = part
    old_top = tops[unit]
    new_top = jnp.maximum(old_top, top)
    keep = jnp.exp2((old_top - new_top) * EXP2_SCALE)
    add = jnp.exp2((top - new_top) * EXP2_SCALE)
    tops[unit] = new_top
    totals[unit] = totals[unit] * keep + total * add
    sums[unit] = sums[unit] * keep + summed * add


def for_groups(count, items, blocks_dev, body):
    def step(group, carry):
        slots = []
        for slot in range(GROUP):
            position = group * GROUP + slot
            code = items[jnp.minimum(position, count - 1)]
            unit = code // CODE
            slots.append(
                (
                    position,
                    position < count,
                    unit,
                    unit // blocks_dev,
                    unit % blocks_dev,
                    code % CODE,
                )
            )
        body(slots)
        return carry

    lax.fori_loop(0, (count + GROUP - 1) // GROUP, step, 0)


def own_kernel(
    blocks_dev,
    lists,
    lengths,
    q_in,
    k_in,
    v_in,
    tops,
    totals,
    sums,
    far_items,
    far_count,
    own_items,
    q_ref,
    k_ref,
    v_ref,
    vt_ref,
    weights_all,
    sems,
):
    copies = [
        pltpu.make_async_copy(source, target, sems.at[index])
        for index, (source, target) in enumerate(((v_in, v_ref), (q_in, q_ref), (k_in, k_ref)))
    ]
    for copy in copies:
        copy.start()
    base = lists[0, 0, 0]

    def plan_unit(unit, counts):
        head = unit // blocks_dev
        local = unit % blocks_dev

        def plan_entry(entry, counts):
            own, far = counts
            block = lists[head, local, entry] - base
            code = unit * CODE
            is_own = jnp.logical_and(block >= 0, block < blocks_dev)

            @pl.when(is_own)
            def _():
                own_items[own] = code + block

            @pl.when(jnp.logical_not(is_own))
            def _():
                far_items[far] = code + jnp.where(block < 0, block + blocks_dev, block)

            mine = is_own.astype(jnp.int32)
            return own + mine, far + 1 - mine

        return lax.fori_loop(0, lengths[head, local], plan_entry, counts)

    zero = jnp.int32(0)
    own, far = lax.fori_loop(0, HEADS * blocks_dev, plan_unit, (zero, zero))
    far_count[0] = far

    def turn(block, carry):
        for head in range(HEADS):
            lanes = slice(head * HEAD_DIM, (head + 1) * HEAD_DIM)
            vt_ref[lanes, aligned(block)] = v_ref[aligned(block), lanes].T
        return carry

    copies[0].wait()
    lax.fori_loop(0, blocks_dev, turn, 0)
    tops[...] = jnp.full(tops.shape, NEVER, jnp.float32)
    totals[...] = jnp.zeros(totals.shape, jnp.float32)
    sums[...] = jnp.zeros(sums.shape, jnp.float32)
    copies[1].wait()
    copies[2].wait()

    def top_body(slots):
        found = []
        for position, live, unit, head, local, block in slots:
            scores = score_tile(
                k_ref[aligned(block), aligned(head)], q_ref[aligned(local), aligned(head)]
            )
            found.append((unit, jnp.max(scores, axis=0, keepdims=True)))
        for unit, top in found:
            tops[unit] = jnp.maximum(tops[unit], top)

    for_groups(own, own_items, blocks_dev, top_body)

    def weights_body(slots):
        found = []
        for position, live, unit, head, local, block in slots:
            scores = score_tile(
                k_ref[aligned(block), aligned(head)], q_ref[aligned(local), aligned(head)]
            )
            top = jnp.where(live, tops[unit], -NEVER)
            weights = jnp.exp2((scores - top) * EXP2_SCALE)
            weights_all[position] = weights.astype(jnp.bfloat16)
            found.append((unit, jnp.sum(weights, axis=0, keepdims=True)))
        for unit, total in found:
            totals[unit] += total

    for_groups(own, own_items, blocks_dev, weights_body)

    def sum_body(slots):
        found = []
        for position, live, unit, head, local, block in slots:
            summed = jnp.dot(
                vt_ref[aligned(head), aligned(block)],
                weights_all[position],
                preferred_element_type=jnp.float32,
            )
            found.append((unit, summed))
        for unit, summed in found:
            sums[unit] += summed

    for_groups(own, own_items, blocks_dev, sum_body)


def middle_kernel(
    blocks_dev,
    far_items,
    far_count,
    q_ref,
    k_low,
    k_high,
    text,
    tops_in,
    totals_in,
    sums_in,
    near_out,
    weights_out,
    k_far,
    tops,
    totals,
    sums,
    near_tops,
    levels,
    item_tops,
    item_totals,
    weights_all,
    sems,
    out_sems,
):
    tokens = k_low.shape[0]
    copies = [
        pltpu.make_async_copy(k_low, k_far.at[pl.ds(0, tokens)], sems.at[0]),
        pltpu.make_async_copy(k_high, k_far.at[pl.ds(tokens, tokens)], sems.at[1]),
    ]
    for copy in copies:
        copy.start()
    tops[...] = tops_in[...]
    totals[...] = totals_in[...]
    sums[...] = sums_in[...]

    def text_head(head, carry):
        keys = text[0, :, aligned(head)]
        values_t = text[1, :, aligned(head)].T
        parts = []
        for pair in range(blocks_dev // 2):
            rows = pl.ds(pair * 2 * BLOCK, 2 * BLOCK)
            parts.append(partial_attention(keys, q_ref[rows, aligned(head)], values_t))
        for pair, (top, total, summed) in enumerate(parts):
            for side in range(2):
                unit = head * blocks_dev + pair * 2 + side
                lanes = slice(side * BLOCK, (side + 1) * BLOCK)
                merge(unit, (top[:, lanes], total[:, lanes], summed[:, lanes]), tops, totals, sums)
        return carry

    lax.fori_loop(0, HEADS, text_head, 0)
    for copy in copies:
        copy.wait()
    near_tops[...] = tops[...]
    count = far_count[0]

    def total_body(slots):
        found = []
        for position, live, unit, head, local, block in slots:
            scores = score_tile(
                k_far[aligned(block), aligned(head)], q_ref[aligned(local), aligned(head)]
            )
            top = jnp.max(scores, axis=0, keepdims=True)
            total = jnp.sum(jnp.exp2((scores - top) * EXP2_SCALE), axis=0, keepdims=True)
            found.append((unit, position, jnp.where(live, top, NEVER), total))
        for unit, position, top, total in found:
            item_tops[position] = top
            item_totals[position] = total
            tops[unit] = jnp.maximum(tops[unit], top)

    for_groups(count, far_items, blocks_dev, total_body)
    totals[...] = totals[...] * jnp.exp2((near_tops[...] - tops[...]) * EXP2_SCALE)

    def fold_body(slots):
        found = []
        for position, live, unit, head, local, block in slots:
            add = jnp.exp2((item_tops[position] - tops[unit]) * EXP2_SCALE)
            found.append((unit, item_totals[position] * add))
        for unit, total in found:
            totals[unit] += total

    for_groups(count, far_items, blocks_dev, fold_body)
    levels[...] = tops[...] * EXP2_SCALE + jnp.log2(totals[...])

    def weights_body(slots):
        for position, live, unit, head, local, block in slots:
            scores = score_tile(
                k_far[aligned(block), aligned(head)], q_ref[aligned(local), aligned(head)]
            )
            level = jnp.where(live, levels[unit], -NEVER)
            weights = jnp.exp2(scores * EXP2_SCALE - level).astype(jnp.bfloat16)
            weights_all[position] = weights.T
        first = pl.multiple_of(slots[0][0], GROUP)
        part = pl.ds(first, GROUP)
        pltpu.make_async_copy(
            weights_all.at[part], weights_out.at[part], out_sems.at[first // GROUP]
        ).start()

    for_groups(count, far_items, blocks_dev, weights_body)

    def near_rows(local, carry):
        for head in range(HEADS):
            unit = head * blocks_dev + local
            factor = jnp.exp2(near_tops[unit] * EXP2_SCALE - levels[unit])
            near_out[aligned(local), head * HEAD_DIM : (head + 1) * HEAD_DIM] = (
                sums[unit] * factor
            ).T
        return carry

    lax.fori_loop(0, blocks_dev, near_rows, 0)

    def settle(group, carry):
        part = pl.ds(pl.multiple_of(group * GROUP, GROUP), GROUP)
        pltpu.make_async_copy(weights_all.at[part], weights_out.at[part], out_sems.at[group]).wait()
        return carry

    lax.fori_loop(0, (count + GROUP - 1) // GROUP, settle, 0)


def last_kernel(
    blocks_dev,
    far_items,
    far_count,
    near,
    weights,
    v_low,
    v_high,
    out_ref,
    v_far,
    total_rows,
    weights_all,
    sems,
    weight_sems,
):
    tokens = v_low.shape[0]
    count = far_count[0]
    groups = (count + GROUP - 1) // GROUP

    def weight_copy(group):
        part = pl.ds(pl.multiple_of(group * GROUP, GROUP), GROUP)
        return pltpu.make_async_copy(weights.at[part], weights_all.at[part], weight_sems.at[group])

    copies = [
        pltpu.make_async_copy(v_low, v_far.at[pl.ds(0, tokens)], sems.at[0]),
        pltpu.make_async_copy(v_high, v_far.at[pl.ds(tokens, tokens)], sems.at[1]),
        pltpu.make_async_copy(near, total_rows, sems.at[2]),
    ]
    for copy in copies:
        copy.start()

    def begin(group, carry):
        weight_copy(group).start()
        return carry

    lax.fori_loop(0, groups, begin, 0)
    for copy in copies:
        copy.wait()

    def body(slots):
        weight_copy(slots[0][0] // GROUP).wait()
        parts = []
        for position, live, unit, head, local, block in slots:
            parts.append(
                jnp.dot(
                    weights_all[position],
                    v_far[aligned(block), aligned(head)],
                    preferred_element_type=jnp.float32,
                )
            )
        for slot, part in zip(slots, parts):
            total_rows[aligned(slot[4]), aligned(slot[3])] += part

    for_groups(count, far_items, blocks_dev, body)
    out_ref[...] = total_rows[...].astype(jnp.bfloat16)


def text_step(text, distance):
    count = lax.axis_size("seq")
    pairs = [(i, i ^ distance) for i in range(count)]
    return jnp.concatenate([text, lax.ppermute(text, "seq", pairs)], axis=1)


def on_device(queries, video_keys, video_values, text_keys, text_values, block_lists, list_lengths):
    tokens = queries.shape[0]
    columns = queries.shape[1]
    blocks_dev = tokens // BLOCK
    count = lax.axis_size("seq")
    assert blocks_dev == REACH and 2 * blocks_dev <= CODE and count & (count - 1) == 0
    units = HEADS * blocks_dev
    longest = block_lists.shape[2]
    forward = [(i, i + 1) for i in range(count - 1)]
    backward = [(target, source) for source, target in forward]

    k_low = lax.ppermute(video_keys, "seq", forward)
    k_high = lax.ppermute(video_keys, "seq", backward)
    text = text_step(jnp.stack([text_keys, text_values], 0), 2)
    v_low = lax.ppermute(video_values, "seq", forward)
    v_high = lax.ppermute(video_values, "seq", backward)
    distance = 4
    while distance < count:
        text = text_step(text, distance)
        distance *= 2
    text = text_step(text, 1)

    smem = pl.BlockSpec(memory_space=pltpu.SMEM)
    vmem = pl.BlockSpec(memory_space=pltpu.VMEM)
    anywhere = pl.BlockSpec(memory_space=pl.ANY)
    stat = (units, 1, BLOCK)
    squares = (units, HEAD_DIM, BLOCK)
    room = -(-units * (longest - 1) // GROUP) * GROUP
    weights_shape = (room, BLOCK, BLOCK)
    params = pltpu.CompilerParams(vmem_limit_bytes=VMEM_BYTES)

    tops, totals, sums, far_items, far_count = pl.pallas_call(
        functools.partial(own_kernel, blocks_dev),
        out_shape=(
            jax.ShapeDtypeStruct(stat, jnp.float32),
            jax.ShapeDtypeStruct(stat, jnp.float32),
            jax.ShapeDtypeStruct(squares, jnp.float32),
            jax.ShapeDtypeStruct((room,), jnp.int32),
            jax.ShapeDtypeStruct((1,), jnp.int32),
        ),
        in_specs=[smem, smem] + [anywhere] * 3,
        out_specs=(vmem, vmem, vmem, smem, smem),
        scratch_shapes=[
            pltpu.SMEM((units * longest,), jnp.int32),
            pltpu.VMEM((tokens, columns), jnp.bfloat16),
            pltpu.VMEM((tokens, columns), jnp.bfloat16),
            pltpu.VMEM((tokens, columns), jnp.bfloat16),
            pltpu.VMEM((columns, tokens), jnp.bfloat16),
            pltpu.VMEM((units * blocks_dev, BLOCK, BLOCK), jnp.bfloat16),
            pltpu.SemaphoreType.DMA((3,)),
        ],
        compiler_params=params,
        cost_estimate=pl.CostEstimate(
            flops=6_000_000_000, bytes_accessed=6_000_000, transcendentals=2_000_000
        ),
        name="own",
    )(block_lists, list_lengths, queries, video_keys, video_values)

    near, weights = pl.pallas_call(
        functools.partial(middle_kernel, blocks_dev),
        out_shape=(
            jax.ShapeDtypeStruct((tokens, columns), jnp.float32),
            jax.ShapeDtypeStruct(weights_shape, jnp.bfloat16),
        ),
        in_specs=[smem, smem, vmem, anywhere, anywhere] + [vmem] * 4,
        out_specs=(vmem, anywhere),
        scratch_shapes=[
            pltpu.VMEM((2 * tokens, columns), jnp.bfloat16),
            pltpu.VMEM(stat, jnp.float32),
            pltpu.VMEM(stat, jnp.float32),
            pltpu.VMEM(squares, jnp.float32),
            pltpu.VMEM(stat, jnp.float32),
            pltpu.VMEM(stat, jnp.float32),
            pltpu.VMEM((room, 1, BLOCK), jnp.float32),
            pltpu.VMEM((room, 1, BLOCK), jnp.float32),
            pltpu.VMEM(weights_shape, jnp.bfloat16),
            pltpu.SemaphoreType.DMA((2,)),
            pltpu.SemaphoreType.DMA((room // GROUP,)),
        ],
        compiler_params=params,
        cost_estimate=pl.CostEstimate(
            flops=8_000_000_000, bytes_accessed=12_000_000, transcendentals=5_000_000
        ),
        name="middle",
    )(far_items, far_count, queries, k_low, k_high, text, tops, totals, sums)

    return pl.pallas_call(
        functools.partial(last_kernel, blocks_dev),
        out_shape=jax.ShapeDtypeStruct((tokens, columns), jnp.bfloat16),
        in_specs=[smem, smem] + [anywhere] * 4,
        out_specs=vmem,
        scratch_shapes=[
            pltpu.VMEM((2 * tokens, columns), jnp.bfloat16),
            pltpu.VMEM((tokens, columns), jnp.float32),
            pltpu.VMEM(weights_shape, jnp.bfloat16),
            pltpu.SemaphoreType.DMA((3,)),
            pltpu.SemaphoreType.DMA((room // GROUP,)),
        ],
        compiler_params=params,
        cost_estimate=pl.CostEstimate(
            flops=1_000_000_000, bytes_accessed=9_000_000, transcendentals=0
        ),
        name="last",
    )(far_items, far_count, near, weights, v_low, v_high)


def solution(mesh):
    in_specs = (
        P(("groups", "seq"), None),
        P(("groups", "seq"), None),
        P(("groups", "seq"), None),
        P(("groups", "seq"), None),
        P(("groups", "seq"), None),
        P(None, ("groups", "seq"), None),
        P(None, ("groups", "seq")),
    )
    out_specs = P(("groups", "seq"), None)
    return jax.shard_map(
        on_device, mesh=mesh, in_specs=in_specs, out_specs=out_specs, check_vma=False
    )
```

profile of v0, /device:TPU:5, one launch (start us, length us, event | category | flops | bytes accessed | tf_op | source)
XLA Modules:
  0.0 76.8 jit_solution(2330345444035329813)
XLA Ops:
  0.0 0.7 pad_maximum_fusion.3
  0.7 1.2 %collective-permute-start.2 = (bf16[2,16,512]{2,1,0:T(8,128)(2,1)S(1)}, bf16[2,16,512]{2,1,0:T(8,128)(2,1)S(1)}, u32[]{:S(2)}, u32[]{:S(2)}) collective-permute-start(bf16[2,16,512]{2,1,0:T(8,128)(2,1)S(1)} %get-tuple-element.19), channel_id=1, source_target_pairs={{0,2},{1,3},{2,0},{3,1},{4,6},{5,7},{6,4},{7,5},{8,10},{9,11},{10,... | collective-permute-start | bytes 98312 | tf_op jit(solution)/shard_map/ppermute | solution.py:364
  2.0 1.6 %collective-permute-done.2 = bf16[2,16,512]{2,1,0:T(8,128)(2,1)S(1)} collective-permute-done((bf16[2,16,512]{2,1,0:T(8,128)(2,1)S(1)}, bf16[2,16,512]{2,1,0:T(8,128)(2,1)S(1)}, u32[]{:S(2)}, u32[]{:S(2)}) %collective-permute-start.2) | collective-permute-done | bytes 32800 | tf_op jit(solution)/shard_map/ppermute | solution.py:364
  3.5 0.7 pad_maximum_fusion.2
  4.2 1.3 %collective-permute-start.3 = (bf16[2,32,512]{2,1,0:T(8,128)(2,1)S(1)}, bf16[2,32,512]{2,1,0:T(8,128)(2,1)S(1)}, u32[]{:S(2)}, u32[]{:S(2)}) collective-permute-start(bf16[2,32,512]{2,1,0:T(8,128)(2,1)S(1)} %pad_maximum_fusion.2), channel_id=1, source_target_pairs={{0,4},{1,5},{2,6},{3,7},{4,0},{5,1},{6,2},{7,3},{8,12},{9,13},{10,... | collective-permute-start | bytes 196616 | tf_op jit(solution)/shard_map/ppermute | solution.py:364
  5.5 5.1 %collective-permute-start = (bf16[1024,512]{1,0:T(8,128)(2,1)}, bf16[1024,512]{1,0:T(8,128)(2,1)S(1)}, u32[]{:S(2)}, u32[]{:S(2)}) collective-permute-start(bf16[1024,512]{1,0:T(8,128)(2,1)} %k_in.1), channel_id=1, source_target_pairs={{0,1},{1,2},{2,3},{3,4},{4,5},{5,6},{6,7},{7,8},{8,9},{9,10},{10,1... | collective-permute-start | bytes 3145736 | tf_op jit(solution)/shard_map/ppermute | solution.py:378
  10.7 1.9 %collective-permute-start.1 = (bf16[1024,512]{1,0:T(8,128)(2,1)}, bf16[1024,512]{1,0:T(8,128)(2,1)}, u32[]{:S(2)}, u32[]{:S(2)}) collective-permute-start(bf16[1024,512]{1,0:T(8,128)(2,1)} %k_in.1), channel_id=1, source_target_pairs={{1,0},{2,1},{3,2},{4,3},{5,4},{6,5},{7,6},{8,7},{9,8},{10,9},{11,1... | collective-permute-start | bytes 3145736 | tf_op jit(solution)/shard_map/ppermute | solution.py:379
  12.6 3.6 %collective-permute-start.6 = (bf16[1024,512]{1,0:T(8,128)(2,1)}, bf16[1024,512]{1,0:T(8,128)(2,1)S(1)}, u32[]{:S(2)}, u32[]{:S(2)}) collective-permute-start(bf16[1024,512]{1,0:T(8,128)(2,1)} %v_in.1), channel_id=1, source_target_pairs={{0,1},{1,2},{2,3},{3,4},{4,5},{5,6},{6,7},{7,8},{8,9},{9,10},{10,1... | collective-permute-start | bytes 3145736 | tf_op jit(solution)/shard_map/ppermute | solution.py:381
  16.2 1.9 %collective-permute-start.7 = (bf16[1024,512]{1,0:T(8,128)(2,1)}, bf16[1024,512]{1,0:T(8,128)(2,1)S(1)}, u32[]{:S(2)}, u32[]{:S(2)}) collective-permute-start(bf16[1024,512]{1,0:T(8,128)(2,1)} %v_in.1), channel_id=1, source_target_pairs={{1,0},{2,1},{3,2},{4,3},{5,4},{6,5},{7,6},{8,7},{9,8},{10,9},{11,1... | collective-permute-start | bytes 3145736 | tf_op jit(solution)/shard_map/ppermute | solution.py:382
  18.2 0.0 collective-permute-done.3
  18.2 0.7 pad_maximum_fusion.1
  18.9 0.0 copy-start.2
  18.9 0.0 copy-start.3
  19.0 2.4 %collective-permute-start.4 = (bf16[2,64,512]{2,1,0:T(8,128)(2,1)S(1)}, bf16[2,64,512]{2,1,0:T(8,128)(2,1)S(1)}, u32[]{:S(2)}, u32[]{:S(2)}) collective-permute-start(bf16[2,64,512]{2,1,0:T(8,128)(2,1)S(1)} %pad_maximum_fusion.1), channel_id=1, source_target_pairs={{0,8},{1,9},{2,10},{3,11},{4,12},{5,13},{6,14},{7,15},{8,0},{9,1},... | collective-permute-start | bytes 393224 | tf_op jit(solution)/shard_map/ppermute | solution.py:364
  21.3 15.7 %own.1 = (f32[32,1,128]{2,1,0:T(1,128)}, f32[32,1,128]{2,1,0:T(1,128)}, f32[32,128,128]{2,1,0:T(8,128)}, s32[256]{0:T(256)}, s32[1]{0:T(128)}) custom-call(s32[4,8,9]{2,1,0:T(8,128)} %lists.1, s32[4,8]{1,0:T(4,128)} %lengths.1, bf16[1024,512]{1,0:T(8,128)(2,1)} %q_ref.1, bf16[1024,512]{1,0:T(8,128)(2,1)} %k_in.1, bf16[1024,512]{1,0:T(8,128)(2,1)} %v_in.1), custom_call_target="tpu_custom_call" | custom-call | flops 6000000000 | bytes 6000000 | tf_op jit(solution)/shard_map/own/pallas_call | solution.py:398
  37.1 0.0 collective-permute-done.4
  37.1 0.0 copy-done.2
  37.1 0.0 copy-done.3
  37.1 9.6 %collective-permute-start.5 = (bf16[2,128,512]{2,1,0:T(8,128)(2,1)S(1)}, bf16[2,128,512]{2,1,0:T(8,128)(2,1)S(1)}, u32[]{:S(2)}, u32[]{:S(2)}) collective-permute-start(bf16[2,128,512]{2,1,0:T(8,128)(2,1)S(1)} %pad_maximum_fusion), channel_id=1, source_target_pairs={{0,1},{1,0},{2,3},{3,2},{4,5},{5,4},{6,7},{7,6},{8,9},{9,8},{10,11... | collective-permute-start | bytes 786440 | tf_op jit(solution)/shard_map/ppermute | solution.py:364
  46.7 1.1 %collective-permute-done.5 = bf16[2,128,512]{2,1,0:T(8,128)(2,1)S(1)} collective-permute-done((bf16[2,128,512]{2,1,0:T(8,128)(2,1)S(1)}, bf16[2,128,512]{2,1,0:T(8,128)(2,1)S(1)}, u32[]{:S(2)}, u32[]{:S(2)}) %collective-permute-start.5) | collective-permute-done | bytes 262176 | tf_op jit(solution)/shard_map/ppermute | solution.py:364
  47.9 0.0 copy-start.4
  47.9 0.0 collective-permute-done.k_low
  47.9 0.0 copy-start.5
  47.9 0.0 collective-permute-done.1.k_high
  47.9 0.8 copy-done.4
  48.7 0.3 copy-done.5
  49.0 18.4 %middle.1 = (f32[1024,512]{1,0:T(8,128)}, bf16[256,128,128]{2,1,0:T(8,128)(2,1)}) custom-call(s32[256]{0:T(256)} %get-tuple-element.12.far_items, s32[1]{0:T(128)} %get-tuple-element.13.far_count, bf16[1024,512]{1,0:T(8,128)(2,1)} %q_ref.1, bf16[1024,512]{1,0:T(8,128)(2,1)} %copy-done.5, bf16[1024,512]{1,0:T(8,128)(2,1)} %collective-permute-done.1.k_high, ...), custom_call_target="tpu_custom_call" | custom-call | flops 8000000000 | bytes 12000000 | tf_op jit(solution)/shard_map/middle/pallas_call | solution.py:425
  67.5 0.0 collective-permute-done.6.v_low
  67.5 0.0 collective-permute-done.7.v_high
  67.5 0.9 %copy-done = bf16[1024,512]{1,0:T(8,128)(2,1)} copy-done((bf16[1024,512]{1,0:T(8,128)(2,1)}, bf16[1024,512]{1,0:T(8,128)(2,1)S(1)}, u32[]{:S(2)}) %copy-start) | copy-done | bytes 1048600
  68.5 0.4 copy-done.1
  68.8 8.0 %last.1 = bf16[1024,512]{1,0:T(8,128)(2,1)} custom-call(s32[256]{0:T(256)} %get-tuple-element.12.far_items, s32[1]{0:T(128)} %get-tuple-element.13.far_count, f32[1024,512]{1,0:T(8,128)} %get-tuple-element.17.near, bf16[256,128,128]{2,1,0:T(8,128)(2,1)} %get-tuple-element.18.weights, bf16[1024,512]{1,0:T(8,128)(2,1)} %copy-done, bf16[1024,512]{1,0:T(8,128)(2,1)} %copy-done.1), custom_call_target="tpu_custom_call" | custom-call | flops 1000000000 | bytes 9000000 | tf_op jit(solution)/shard_map/last/pallas_call | solution.py:453
  (7 shorter events, 0.1 us)
Async XLA Ops:
  0.7 2.8 %collective-permute-start.2 = (bf16[2,16,512]{2,1,0:T(8,128)(2,1)S(1)}, bf16[2,16,512]{2,1,0:T(8,128)(2,1)S(1)}, u32[]{:S(2)}, u32[]{:S(2)}) collective-permute-start(bf16[2,16,512]{2,1,0:T(8,128)(2,1)S(1)} %get-tuple-element.19), channel_id=1, source_target_pairs={{0,2},{1,3},{2,0},{3,1},{4,6},{5,7},{6,4},{7,5},{8,10},{9,11},{10,... | collective-permute-start | bytes 98312 | tf_op jit(solution)/shard_map/ppermute | solution.py:364
  4.2 13.9 %collective-permute-start.3 = (bf16[2,32,512]{2,1,0:T(8,128)(2,1)S(1)}, bf16[2,32,512]{2,1,0:T(8,128)(2,1)S(1)}, u32[]{:S(2)}, u32[]{:S(2)}) collective-permute-start(bf16[2,32,512]{2,1,0:T(8,128)(2,1)S(1)} %pad_maximum_fusion.2), channel_id=1, source_target_pairs={{0,4},{1,5},{2,6},{3,7},{4,0},{5,1},{6,2},{7,3},{8,12},{9,13},{10,... | collective-permute-start | bytes 196616 | tf_op jit(solution)/shard_map/ppermute | solution.py:364
  5.5 42.4 %collective-permute-start = (bf16[1024,512]{1,0:T(8,128)(2,1)}, bf16[1024,512]{1,0:T(8,128)(2,1)S(1)}, u32[]{:S(2)}, u32[]{:S(2)}) collective-permute-start(bf16[1024,512]{1,0:T(8,128)(2,1)} %k_in.1), channel_id=1, source_target_pairs={{0,1},{1,2},{2,3},{3,4},{4,5},{5,6},{6,7},{7,8},{8,9},{9,10},{10,1... | collective-permute-start | bytes 3145736 | tf_op jit(solution)/shard_map/ppermute | solution.py:378
  10.7 37.3 %collective-permute-start.1 = (bf16[1024,512]{1,0:T(8,128)(2,1)}, bf16[1024,512]{1,0:T(8,128)(2,1)}, u32[]{:S(2)}, u32[]{:S(2)}) collective-permute-start(bf16[1024,512]{1,0:T(8,128)(2,1)} %k_in.1), channel_id=1, source_target_pairs={{1,0},{2,1},{3,2},{4,3},{5,4},{6,5},{7,6},{8,7},{9,8},{10,9},{11,1... | collective-permute-start | bytes 3145736 | tf_op jit(solution)/shard_map/ppermute | solution.py:379
  12.6 54.9 %collective-permute-start.6 = (bf16[1024,512]{1,0:T(8,128)(2,1)}, bf16[1024,512]{1,0:T(8,128)(2,1)S(1)}, u32[]{:S(2)}, u32[]{:S(2)}) collective-permute-start(bf16[1024,512]{1,0:T(8,128)(2,1)} %v_in.1), channel_id=1, source_target_pairs={{0,1},{1,2},{2,3},{3,4},{4,5},{5,6},{6,7},{7,8},{8,9},{9,10},{10,1... | collective-permute-start | bytes 3145736 | tf_op jit(solution)/shard_map/ppermute | solution.py:381
  16.2 51.3 %collective-permute-start.7 = (bf16[1024,512]{1,0:T(8,128)(2,1)}, bf16[1024,512]{1,0:T(8,128)(2,1)S(1)}, u32[]{:S(2)}, u32[]{:S(2)}) collective-permute-start(bf16[1024,512]{1,0:T(8,128)(2,1)} %v_in.1), channel_id=1, source_target_pairs={{1,0},{2,1},{3,2},{4,3},{5,4},{6,5},{7,6},{8,7},{9,8},{10,9},{11,1... | collective-permute-start | bytes 3145736 | tf_op jit(solution)/shard_map/ppermute | solution.py:382
  18.9 18.2 %copy-start.2 = (bf16[16,512]{1,0:T(8,128)(2,1)S(1)}, bf16[16,512]{1,0:T(8,128)(2,1)}, u32[]{:S(2)}) copy-start(bf16[16,512]{1,0:T(8,128)(2,1)} %param.11) | copy-start | bytes 49156
  18.9 18.2 %copy-start.3 = (bf16[16,512]{1,0:T(8,128)(2,1)S(1)}, bf16[16,512]{1,0:T(8,128)(2,1)}, u32[]{:S(2)}) copy-start(bf16[16,512]{1,0:T(8,128)(2,1)} %param.10) | copy-start | bytes 49156
  19.0 18.1 %collective-permute-start.4 = (bf16[2,64,512]{2,1,0:T(8,128)(2,1)S(1)}, bf16[2,64,512]{2,1,0:T(8,128)(2,1)S(1)}, u32[]{:S(2)}, u32[]{:S(2)}) collective-permute-start(bf16[2,64,512]{2,1,0:T(8,128)(2,1)S(1)} %pad_maximum_fusion.1), channel_id=1, source_target_pairs={{0,8},{1,9},{2,10},{3,11},{4,12},{5,13},{6,14},{7,15},{8,0},{9,1},... | collective-permute-start | bytes 393224 | tf_op jit(solution)/shard_map/ppermute | solution.py:364
  37.1 10.7 %collective-permute-start.5 = (bf16[2,128,512]{2,1,0:T(8,128)(2,1)S(1)}, bf16[2,128,512]{2,1,0:T(8,128)(2,1)S(1)}, u32[]{:S(2)}, u32[]{:S(2)}) collective-permute-start(bf16[2,128,512]{2,1,0:T(8,128)(2,1)S(1)} %pad_maximum_fusion), channel_id=1, source_target_pairs={{0,1},{1,0},{2,3},{3,2},{4,5},{5,4},{6,7},{7,6},{8,9},{9,8},{10,11... | collective-permute-start | bytes 786440 | tf_op jit(solution)/shard_map/ppermute | solution.py:364
  47.9 0.8 %copy-start.4 = (bf16[2,256,512]{2,1,0:T(8,128)(2,1)}, bf16[2,256,512]{2,1,0:T(8,128)(2,1)S(1)}, u32[]{:S(2)}) copy-start(bf16[2,256,512]{2,1,0:T(8,128)(2,1)S(1)} %constant_dynamic-update-slice_fusion.text) | copy-start | bytes 1572868
  47.9 1.1 %copy-start.5 = (bf16[1024,512]{1,0:T(8,128)(2,1)}, bf16[1024,512]{1,0:T(8,128)(2,1)S(1)}, u32[]{:S(2)}) copy-start(bf16[1024,512]{1,0:T(8,128)(2,1)S(1)} %collective-permute-done.k_low) | copy-start | bytes 3145732
  67.5 1.0 %copy-start = (bf16[1024,512]{1,0:T(8,128)(2,1)}, bf16[1024,512]{1,0:T(8,128)(2,1)S(1)}, u32[]{:S(2)}) copy-start(bf16[1024,512]{1,0:T(8,128)(2,1)S(1)} %collective-permute-done.6.v_low) | copy-start | bytes 3145732
  67.5 1.3 %copy-start.1 = (bf16[1024,512]{1,0:T(8,128)(2,1)}, bf16[1024,512]{1,0:T(8,128)(2,1)S(1)}, u32[]{:S(2)}) copy-start(bf16[1024,512]{1,0:T(8,128)(2,1)S(1)} %collective-permute-done.7.v_high) | copy-start | bytes 3145732
where the time goes:
time: 76.4 us; the launch traced here: 76.8 us
  Pallas kernels  42.1 us (55%)
  starting transfers between devices  27 us (35%)
  waiting for transfers between devices  2.7 us (4%)
  local copies, waits for them, and re-layouts  2.47 us (3%)
  other arithmetic  2.25 us (3%)
    pallas_call x1, Pallas kernels, on_device(): pl.pallas_call(functools.partial(middle_kernel, blocks_dev), out_shape=(j...  18.4 us
    pallas_call x1, Pallas kernels, on_device(): pl.pallas_call(functools.partial(own_kernel, blocks_dev), out_shape=(jax....  15.7 us
    ppermute x4, starting transfers between devices, text_step(): return jnp.concatenate([text, lax.ppermute(text, 'seq', pairs)], axis=1)  14.5 us
    pallas_call x1, Pallas kernels, on_device(): pl.pallas_call(functools.partial(last_kernel, blocks_dev), out_shape=jax....  7.95 us
    ppermute x1, starting transfers between devices, on_device(): k_low = lax.ppermute(video_keys, 'seq', forward)  5.1 us
    ppermute x1, starting transfers between devices, on_device(): v_low = lax.ppermute(video_values, 'seq', forward)  3.64 us
    ppermute x4, waiting for transfers between devices, text_step(): return jnp.concatenate([text, lax.ppermute(text, 'seq', pairs)], axis=1)  2.69 us
    unnamed x15, local copies, waits for them, and re-layouts  2.45 us
  transfers between devices with their start and end apart: 8, of which 2 were waited for; matrix products, arithmetic and copies ran while one was open for 1% of the time, Pallas kernels for 45%

commit v1 on v0

--- a/solution.py
+++ b/solution.py
@@ -16,7 +16,7 @@
 EXP2_SCALE = HEAD_DIM ** (-0.5) * math.log2(math.e)
 NEVER = -1e30
 NT = (((1,), (1,)), ((), ()))
-VMEM_BYTES = 60 * 1024 * 1024
+VMEM_BYTES = 63 * 1024 * 1024
 CODE = 64
 
 
@@ -26,26 +26,6 @@
 
 def score_tile(keys, query_rows):
     return lax.dot_general(keys, query_rows, NT, preferred_element_type=jnp.float32)
-
-
-def partial_attention(keys, query_rows, values_t):
-    scores = score_tile(keys, query_rows)
-    top = jnp.max(scores, axis=0, keepdims=True)
-    weights = jnp.exp2((scores - top) * EXP2_SCALE)
-    total = jnp.sum(weights, axis=0, keepdims=True)
-    summed = jnp.dot(values_t, weights.astype(jnp.bfloat16), preferred_element_type=jnp.float32)
-    return top, total, summed
-
-
-def merge(unit, part, tops, totals, sums):
-    top, total, summed = part
-    old_top = tops[unit]
-    new_top = jnp.maximum(old_top, top)
-    keep = jnp.exp2((old_top - new_top) * EXP2_SCALE)
-    add = jnp.exp2((top - new_top) * EXP2_SCALE)
-    tops[unit] = new_top
-    totals[unit] = totals[unit] * keep + total * add
-    sums[unit] = sums[unit] * keep + summed * add
 
 
 def for_groups(count, items, blocks_dev, body):
@@ -71,60 +51,122 @@
     lax.fori_loop(0, (count + GROUP - 1) // GROUP, step, 0)
 
 
-def own_kernel(
+def text_kernel(
     blocks_dev,
     lists,
     lengths,
     q_in,
-    k_in,
-    v_in,
+    text_in,
+    own_items,
+    far_items,
+    counts,
     tops,
     totals,
     sums,
-    far_items,
-    far_count,
+    q_ref,
+    text,
+    weights_all,
+    sems,
+):
+    copies = [
+        pltpu.make_async_copy(text_in, text, sems.at[0]),
+        pltpu.make_async_copy(q_in, q_ref, sems.at[1]),
+    ]
+    for copy in copies:
+        copy.start()
+    base = lists[0, 0, 0]
+
+    def plan_unit(unit, carry):
+        head = unit // blocks_dev
+        local = unit % blocks_dev
+
+        def plan_entry(entry, carry):
+            own, far = carry
+            block = lists[head, local, entry] - base
+            code = unit * CODE
+            is_own = jnp.logical_and(block >= 0, block < blocks_dev)
+
+            @pl.when(is_own)
+            def _():
+                own_items[own] = code + block
+
+            @pl.when(jnp.logical_not(is_own))
+            def _():
+                far_items[far] = code + jnp.where(block < 0, block + blocks_dev, block)
+
+            mine = is_own.astype(jnp.int32)
+            return own + mine, far + 1 - mine
+
+        return lax.fori_loop(0, lengths[head, local], plan_entry, carry)
+
+    zero = jnp.int32(0)
+    own, far = lax.fori_loop(0, HEADS * blocks_dev, plan_unit, (zero, zero))
+    counts[0] = own
+    counts[1] = far
+    for copy in copies:
+        copy.wait()
+    pairs = blocks_dev // 2
+
+    def weights_head(head, carry):
+        keys = text[0, :, aligned(head)]
+        for pair in range(pairs):
+            rows = pl.ds(pair * 2 * BLOCK, 2 * BLOCK)
+            scores = score_tile(keys, q_ref[rows, aligned(head)])
+            top = jnp.max(scores, axis=0, keepdims=True)
+            weights = jnp.exp2((scores - top) * EXP2_SCALE)
+            weights_all[head * pairs + pair] = weights.astype(jnp.bfloat16)
+            total = jnp.sum(weights, axis=0, keepdims=True)
+            for side in range(2):
+                unit = head * blocks_dev + pair * 2 + side
+                lanes = slice(side * BLOCK, (side + 1) * BLOCK)
+                tops[unit] = top[:, lanes]
+                totals[unit] = total[:, lanes]
+        return carry
+
+    lax.fori_loop(0, HEADS, weights_head, 0)
+
+    def sums_head(head, carry):
+        values_t = text[1, :, aligned(head)].T
+        for pair in range(pairs):
+            summed = jnp.dot(
+                values_t, weights_all[head * pairs + pair], preferred_element_type=jnp.float32
+            )
+            for side in range(2):
+                unit = head * blocks_dev + pair * 2 + side
+                sums[unit] = summed[:, side * BLOCK : (side + 1) * BLOCK]
+        return carry
+
+    lax.fori_loop(0, HEADS, sums_head, 0)
+
+
+def own_kernel(
+    blocks_dev,
     own_items,
+    counts,
+    q_in,
+    k_in,
+    v_in,
+    sums_in,
+    text_tops,
+    text_totals,
+    tops,
+    totals,
+    sums,
     q_ref,
     k_ref,
     v_ref,
     vt_ref,
+    scores_all,
     weights_all,
     sems,
 ):
     copies = [
         pltpu.make_async_copy(source, target, sems.at[index])
-        for index, (source, target) in enumerate(((v_in, v_ref), (q_in, q_ref), (k_in, k_ref)))
+        for index, (source, target) in enumerate(((q_in, q_ref), (k_in, k_ref), (v_in, v_ref), (sums_in, sums)))
     ]
     for copy in copies:
         copy.start()
-    base = lists[0, 0, 0]
-
-    def plan_unit(unit, counts):
-        head = unit // blocks_dev
-        local = unit % blocks_dev
-
-        def plan_entry(entry, counts):
-            own, far = counts
-            block = lists[head, local, entry] - base
-            code = unit * CODE
-            is_own = jnp.logical_and(block >= 0, block < blocks_dev)
-
-            @pl.when(is_own)
-            def _():
-                own_items[own] = code + block
-
-            @pl.when(jnp.logical_not(is_own))
-            def _():
-                far_items[far] = code + jnp.where(block < 0, block + blocks_dev, block)
-
-            mine = is_own.astype(jnp.int32)
-            return own + mine, far + 1 - mine
-
-        return lax.fori_loop(0, lengths[head, local], plan_entry, counts)
-
-    zero = jnp.int32(0)
-    own, far = lax.fori_loop(0, HEADS * blocks_dev, plan_unit, (zero, zero))
-    far_count[0] = far
+    own = counts[0]
 
     def turn(block, carry):
         for head in range(HEADS):
@@ -132,13 +174,9 @@
             vt_ref[lanes, aligned(block)] = v_ref[aligned(block), lanes].T
         return carry
 
+    tops[...] = text_tops[...]
     copies[0].wait()
-    lax.fori_loop(0, blocks_dev, turn, 0)
-    tops[...] = jnp.full(tops.shape, NEVER, jnp.float32)
-    totals[...] = jnp.zeros(totals.shape, jnp.float32)
-    sums[...] = jnp.zeros(sums.shape, jnp.float32)
     copies[1].wait()
-    copies[2].wait()
 
     def top_body(slots):
         found = []
@@ -146,20 +184,22 @@
             scores = score_tile(
                 k_ref[aligned(block), aligned(head)], q_ref[aligned(local), aligned(head)]
             )
+            scores_all[position] = scores
             found.append((unit, jnp.max(scores, axis=0, keepdims=True)))
         for unit, top in found:
             tops[unit] = jnp.maximum(tops[unit], top)
 
     for_groups(own, own_items, blocks_dev, top_body)
+    factor = jnp.exp2((text_tops[...] - tops[...]) * EXP2_SCALE)
+    totals[...] = text_totals[...] * factor
+    copies[3].wait()
+    sums[...] = sums[...] * factor
 
     def weights_body(slots):
         found = []
         for position, live, unit, head, local, block in slots:
-            scores = score_tile(
-                k_ref[aligned(block), aligned(head)], q_ref[aligned(local), aligned(head)]
-            )
             top = jnp.where(live, tops[unit], -NEVER)
-            weights = jnp.exp2((scores - top) * EXP2_SCALE)
+            weights = jnp.exp2((scores_all[position] - top) * EXP2_SCALE)
             weights_all[position] = weights.astype(jnp.bfloat16)
             found.append((unit, jnp.sum(weights, axis=0, keepdims=True)))
         for unit, total in found:
@@ -179,30 +219,30 @@
         for unit, summed in found:
             sums[unit] += summed
 
+    copies[2].wait()
+    lax.fori_loop(0, blocks_dev, turn, 0)
     for_groups(own, own_items, blocks_dev, sum_body)
 
 
 def middle_kernel(
     blocks_dev,
     far_items,
-    far_count,
+    counts,
     q_ref,
     k_low,
     k_high,
-    text,
-    tops_in,
-    totals_in,
-    sums_in,
+    near_tops,
+    near_totals,
+    sums,
     near_out,
     weights_out,
     k_far,
     tops,
     totals,
-    sums,
-    near_tops,
     levels,
     item_tops,
     item_totals,
+    scores_all,
     weights_all,
     sems,
     out_sems,
@@ -214,29 +254,11 @@
     ]
     for copy in copies:
         copy.start()
-    tops[...] = tops_in[...]
-    totals[...] = totals_in[...]
-    sums[...] = sums_in[...]
-
-    def text_head(head, carry):
-        keys = text[0, :, aligned(head)]
-        values_t = text[1, :, aligned(head)].T
-        parts = []
-        for pair in range(blocks_dev // 2):
-            rows = pl.ds(pair * 2 * BLOCK, 2 * BLOCK)
-            parts.append(partial_attention(keys, q_ref[rows, aligned(head)], values_t))
-        for pair, (top, total, summed) in enumerate(parts):
-            for side in range(2):
-                unit = head * blocks_dev + pair * 2 + side
-                lanes = slice(side * BLOCK, (side + 1) * BLOCK)
-                merge(unit, (top[:, lanes], total[:, lanes], summed[:, lanes]), tops, totals, sums)
-        return carry
-
-    lax.fori_loop(0, HEADS, text_head, 0)
+    tops[...] = near_tops[...]
+    totals[...] = near_totals[...]
     for copy in copies:
         copy.wait()
-    near_tops[...] = tops[...]
-    count = far_count[0]
+    count = counts[1]
 
     def total_body(slots):
         found = []
@@ -246,6 +268,7 @@
             )
             top = jnp.max(scores, axis=0, keepdims=True)
             total = jnp.sum(jnp.exp2((scores - top) * EXP2_SCALE), axis=0, keepdims=True)
+            scores_all[position] = scores
             found.append((unit, position, jnp.where(live, top, NEVER), total))
         for unit, position, top, total in found:
             item_tops[position] = top
@@ -268,11 +291,8 @@
 
     def weights_body(slots):
         for position, live, unit, head, local, block in slots:
-            scores = score_tile(
-                k_far[aligned(block), aligned(head)], q_ref[aligned(local), aligned(head)]
-            )
             level = jnp.where(live, levels[unit], -NEVER)
-            weights = jnp.exp2(scores * EXP2_SCALE - level).astype(jnp.bfloat16)
+            weights = jnp.exp2(scores_all[position] * EXP2_SCALE - level).astype(jnp.bfloat16)
             weights_all[position] = weights.T
         first = pl.multiple_of(slots[0][0], GROUP)
         part = pl.ds(first, GROUP)
@@ -304,7 +324,7 @@
 def last_kernel(
     blocks_dev,
     far_items,
-    far_count,
+    counts,
     near,
     weights,
     v_low,
@@ -317,7 +337,7 @@
     weight_sems,
 ):
     tokens = v_low.shape[0]
-    count = far_count[0]
+    count = counts[1]
     groups = (count + GROUP - 1) // GROUP
 
     def weight_copy(group):
@@ -358,10 +378,12 @@
     out_ref[...] = total_rows[...].astype(jnp.bfloat16)
 
 
-def text_step(text, distance):
+def text_step(text, distances):
     count = lax.axis_size("seq")
-    pairs = [(i, i ^ distance) for i in range(count)]
-    return jnp.concatenate([text, lax.ppermute(text, "seq", pairs)], axis=1)
+    parts = [text]
+    for distance in distances:
+        parts.append(lax.ppermute(text, "seq", [(i, i ^ distance) for i in range(count)]))
+    return jnp.concatenate(parts, axis=1)
 
 
 def on_device(queries, video_keys, video_values, text_keys, text_values, block_lists, list_lengths):
@@ -375,17 +397,6 @@
     forward = [(i, i + 1) for i in range(count - 1)]
     backward = [(target, source) for source, target in forward]
 
-    k_low = lax.ppermute(video_keys, "seq", forward)
-    k_high = lax.ppermute(video_keys, "seq", backward)
-    text = text_step(jnp.stack([text_keys, text_values], 0), 2)
-    v_low = lax.ppermute(video_values, "seq", forward)
-    v_high = lax.ppermute(video_values, "seq", backward)
-    distance = 4
-    while distance < count:
-        text = text_step(text, distance)
-        distance *= 2
-    text = text_step(text, 1)
-
     smem = pl.BlockSpec(memory_space=pltpu.SMEM)
     vmem = pl.BlockSpec(memory_space=pltpu.VMEM)
     anywhere = pl.BlockSpec(memory_space=pl.ANY)
@@ -395,32 +406,75 @@
     weights_shape = (room, BLOCK, BLOCK)
     params = pltpu.CompilerParams(vmem_limit_bytes=VMEM_BYTES)
 
-    tops, totals, sums, far_items, far_count = pl.pallas_call(
+    text = text_step(jnp.stack([text_keys, text_values], 0), (2,))
+    keys, text = lax.optimization_barrier((video_keys, text))
+    k_low = lax.ppermute(keys, "seq", forward)
+    k_high = lax.ppermute(keys, "seq", backward)
+    text = text_step(text, (4, 8, 12) if count >= 16 else (4,) if count == 8 else ())
+    distance = 16
+    while distance < count:
+        text = text_step(text, (distance,))
+        distance *= 2
+    text = text_step(text, (1,))
+
+    own_items, far_items, counts, text_tops, text_totals, text_sums = pl.pallas_call(
+        functools.partial(text_kernel, blocks_dev),
+        out_shape=(
+            jax.ShapeDtypeStruct((units * blocks_dev,), jnp.int32),
+            jax.ShapeDtypeStruct((room,), jnp.int32),
+            jax.ShapeDtypeStruct((2,), jnp.int32),
+            jax.ShapeDtypeStruct(stat, jnp.float32),
+            jax.ShapeDtypeStruct(stat, jnp.float32),
+            jax.ShapeDtypeStruct(squares, jnp.float32),
+        ),
+        in_specs=[smem, smem, anywhere, anywhere],
+        out_specs=(smem, smem, smem, vmem, vmem, vmem),
+        scratch_shapes=[
+            pltpu.VMEM((tokens, columns), jnp.bfloat16),
+            pltpu.VMEM(text.shape, jnp.bfloat16),
+            pltpu.VMEM((units // 2, text.shape[1], 2 * BLOCK), jnp.bfloat16),
+            pltpu.SemaphoreType.DMA((2,)),
+        ],
+        compiler_params=params,
+        cost_estimate=pl.CostEstimate(flops=1_000_000, bytes_accessed=10_000, transcendentals=0),
+        name="text",
+    )(block_lists, list_lengths, queries, text)
+
+    values, own_items = lax.optimization_barrier((video_values, own_items))
+    v_low = lax.ppermute(values, "seq", forward)
+    v_high = lax.ppermute(values, "seq", backward)
+
+    tops, totals, sums = pl.pallas_call(
         functools.partial(own_kernel, blocks_dev),
         out_shape=(
             jax.ShapeDtypeStruct(stat, jnp.float32),
             jax.ShapeDtypeStruct(stat, jnp.float32),
             jax.ShapeDtypeStruct(squares, jnp.float32),
-            jax.ShapeDtypeStruct((room,), jnp.int32),
-            jax.ShapeDtypeStruct((1,), jnp.int32),
         ),
-        in_specs=[smem, smem] + [anywhere] * 3,
-        out_specs=(vmem, vmem, vmem, smem, smem),
+        in_specs=[smem, smem] + [anywhere] * 4 + [vmem] * 2,
+        out_specs=(vmem, vmem, vmem),
         scratch_shapes=[
-            pltpu.SMEM((units * longest,), jnp.int32),
             pltpu.VMEM((tokens, columns), jnp.bfloat16),
             pltpu.VMEM((tokens, columns), jnp.bfloat16),
             pltpu.VMEM((tokens, columns), jnp.bfloat16),
             pltpu.VMEM((columns, tokens), jnp.bfloat16),
+            pltpu.VMEM((units * blocks_dev, BLOCK, BLOCK), jnp.float32),
             pltpu.VMEM((units * blocks_dev, BLOCK, BLOCK), jnp.bfloat16),
-            pltpu.SemaphoreType.DMA((3,)),
+            pltpu.SemaphoreType.DMA((4,)),
         ],
         compiler_params=params,
-        cost_estimate=pl.CostEstimate(
-            flops=6_000_000_000, bytes_accessed=6_000_000, transcendentals=2_000_000
-        ),
+        cost_estimate=pl.CostEstimate(flops=1_000_000, bytes_accessed=10_000, transcendentals=0),
         name="own",
-    )(block_lists, list_lengths, queries, video_keys, video_values)
+    )(
+        own_items,
+        counts,
+        queries,
+        video_keys,
+        video_values,
+        text_sums,
+        text_tops,
+        text_totals,
+    )
 
     near, weights = pl.pallas_call(
         functools.partial(middle_kernel, blocks_dev),
@@ -428,27 +482,26 @@
             jax.ShapeDtypeStruct((tokens, columns), jnp.float32),
             jax.ShapeDtypeStruct(weights_shape, jnp.bfloat16),
         ),
-        in_specs=[smem, smem, vmem, anywhere, anywhere] + [vmem] * 4,
+        in_specs=[smem, smem, vmem, anywhere, anywhere] + [vmem] * 3,
         out_specs=(vmem, anywhere),
         scratch_shapes=[
             pltpu.VMEM((2 * tokens, columns), jnp.bfloat16),
             pltpu.VMEM(stat, jnp.float32),
             pltpu.VMEM(stat, jnp.float32),
-            pltpu.VMEM(squares, jnp.float32),
-            pltpu.VMEM(stat, jnp.float32),
             pltpu.VMEM(stat, jnp.float32),
             pltpu.VMEM((room, 1, BLOCK), jnp.float32),
             pltpu.VMEM((room, 1, BLOCK), jnp.float32),
+            pltpu.VMEM(weights_shape, jnp.float32),
             pltpu.VMEM(weights_shape, jnp.bfloat16),
             pltpu.SemaphoreType.DMA((2,)),
             pltpu.SemaphoreType.DMA((room // GROUP,)),
         ],
         compiler_params=params,
         cost_estimate=pl.CostEstimate(
-            flops=8_000_000_000, bytes_accessed=12_000_000, transcendentals=5_000_000
+            flops=1_000_000, bytes_accessed=10_000, transcendentals=0
         ),
         name="middle",
-    )(far_items, far_count, queries, k_low, k_high, text, tops, totals, sums)
+    )(far_items, counts, queries, k_low, k_high, tops, totals, sums)
 
     return pl.pallas_call(
         functools.partial(last_kernel, blocks_dev),
@@ -467,7 +520,7 @@
             flops=1_000_000_000, bytes_accessed=9_000_000, transcendentals=0
         ),
         name="last",
-    )(far_items, far_count, near, weights, v_low, v_high)
+    )(far_items, counts, near, weights, v_low, v_high)
 
 
 def solution(mesh):

time: 76.4 us -> 68.2 us (0.89)
  the two profiles are of different devices: /device:TPU:5 before, /device:TPU:25 now
where the time goes in v1:
time: 68.2 us; the launch traced here: 67.6 us
  Pallas kernels  36.5 us (54%)
  starting transfers between devices  18.4 us (27%)
  waiting for transfers between devices  10.2 us (15%)
  other arithmetic  1.5 us (2%)
  local copies, waits for them, and re-layouts  0.83 us (1%)
    pallas_call x1, Pallas kernels, on_device(): pl.pallas_call(functools.partial(own_kernel, blocks_dev), out_shape=(jax....  11.2 us
    pallas_call x1, Pallas kernels, on_device(): pl.pallas_call(functools.partial(middle_kernel, blocks_dev), out_shape=(j...  10.8 us
    pallas_call x1, Pallas kernels, on_device(): pl.pallas_call(functools.partial(text_kernel, blocks_dev), out_shape=(jax...  7.65 us
    ppermute x1, waiting for transfers between devices, on_device(): k_high = lax.ppermute(keys, 'seq', backward)  7.1 us
    pallas_call x1, Pallas kernels, on_device(): pl.pallas_call(functools.partial(last_kernel, blocks_dev), out_shape=jax....  6.78 us
    ppermute x5, starting transfers between devices, text_step(): lax.ppermute(text, 'seq', [(i, i ^ distance) for i in range(count)])  6.36 us
    ppermute x1, starting transfers between devices, on_device(): k_low = lax.ppermute(keys, 'seq', forward)  5.66 us
    ppermute x5, waiting for transfers between devices, text_step(): lax.ppermute(text, 'seq', [(i, i ^ distance) for i in range(count)])  2.69 us
  transfers between devices with their start and end apart: 9, of which 4 were waited for; matrix products, arithmetic and copies ran while one was open for 0% of the time, Pallas kernels for 44%

profile of v1, /device:TPU:25, one launch (start us, length us, event | category | flops | bytes accessed | tf_op | source)
XLA Modules:
  0.0 67.6 jit_solution(2516487595295338687)
XLA Ops:
  0.0 0.7 %pad_maximum_fusion.2 = bf16[2,16,512]{2,1,0:T(8,128)(2,1)S(1)} fusion(bf16[1,16,512]{2,1,0:T(8,128)(2,1)} %bitcast.2, bf16[1,16,512]{2,1,0:T(8,128)(2,1)} %bitcast.4), kind=kLoop, calls=%fused_computation.2 | loop fusion | flops 16384 | bytes 65536 | tf_op jit(solution)/shard_map/stack | solution.py:409
  0.7 1.2 %collective-permute-start = (bf16[2,16,512]{2,1,0:T(8,128)(2,1)S(1)}, bf16[2,16,512]{2,1,0:T(8,128)(2,1)S(1)}, u32[]{:S(2)}, u32[]{:S(2)}) collective-permute-start(bf16[2,16,512]{2,1,0:T(8,128)(2,1)S(1)} %pad_maximum_fusion.2), channel_id=1, source_target_pairs={{0,2},{1,3},{2,0},{3,1},{4,6},{5,7},{6,4},{7,5},{8,10},{9,11},{10,... | collective-permute-start | bytes 98312 | tf_op jit(solution)/shard_map/ppermute | solution.py:385
  2.0 1.6 %collective-permute-done = bf16[2,16,512]{2,1,0:T(8,128)(2,1)S(1)} collective-permute-done((bf16[2,16,512]{2,1,0:T(8,128)(2,1)S(1)}, bf16[2,16,512]{2,1,0:T(8,128)(2,1)S(1)}, u32[]{:S(2)}, u32[]{:S(2)}) %collective-permute-start) | collective-permute-done | bytes 32800 | tf_op jit(solution)/shard_map/ppermute | solution.py:385
  3.5 0.7 %pad_maximum_fusion.1 = bf16[2,32,512]{2,1,0:T(8,128)(2,1)S(1)} fusion(bf16[2,16,512]{2,1,0:T(8,128)(2,1)S(1)} %collective-permute-done, bf16[1,16,512]{2,1,0:T(8,128)(2,1)} %bitcast.3, bf16[1,16,512]{2,1,0:T(8,128)(2,1)} %bitcast.5), kind=kLoop, calls=%fused_computation.1 | loop fusion | flops 196608 | bytes 131072 | tf_op jit(solution)/shard_map/concatenate | solution.py:386
  4.2 0.2 collective-permute-start.1
  4.4 0.0 collective-permute-start.2
  4.4 3.4 %collective-permute-start.3 = (bf16[2,32,512]{2,1,0:T(8,128)(2,1)S(1)}, bf16[2,32,512]{2,1,0:T(8,128)(2,1)S(1)}, u32[]{:S(2)}, u32[]{:S(2)}) collective-permute-start(bf16[2,32,512]{2,1,0:T(8,128)(2,1)S(1)} %pad_maximum_fusion.1), channel_id=1, source_target_pairs={{0,12},{1,13},{2,14},{3,15},{4,8},{5,9},{6,10},{7,11},{8,4},{9,5},... | collective-permute-start | bytes 196616 | tf_op jit(solution)/shard_map/ppermute | solution.py:385
  7.8 5.7 %collective-permute-start.5 = (bf16[1024,512]{1,0:T(8,128)(2,1)}, bf16[1024,512]{1,0:T(8,128)(2,1)}, u32[]{:S(2)}, u32[]{:S(2)}) collective-permute-start(bf16[1024,512]{1,0:T(8,128)(2,1)} %k_in.1), channel_id=1, source_target_pairs={{0,1},{1,2},{2,3},{3,4},{4,5},{5,6},{6,7},{7,8},{8,9},{9,10},{10,1... | collective-permute-start | bytes 3145736 | tf_op jit(solution)/shard_map/ppermute | solution.py:411
  13.5 1.9 %collective-permute-start.6 = (bf16[1024,512]{1,0:T(8,128)(2,1)}, bf16[1024,512]{1,0:T(8,128)(2,1)}, u32[]{:S(2)}, u32[]{:S(2)}) collective-permute-start(bf16[1024,512]{1,0:T(8,128)(2,1)} %k_in.1), channel_id=1, source_target_pairs={{1,0},{2,1},{3,2},{4,3},{5,4},{6,5},{7,6},{8,7},{9,8},{10,9},{11,1... | collective-permute-start | bytes 3145736 | tf_op jit(solution)/shard_map/ppermute | solution.py:412
  15.4 0.0 collective-permute-done.1
  15.4 0.0 collective-permute-done.2
  15.4 0.0 collective-permute-done.3
  15.5 1.6 %collective-permute-start.4 = (bf16[2,128,512]{2,1,0:T(8,128)(2,1)S(1)}, bf16[2,128,512]{2,1,0:T(8,128)(2,1)S(1)}, u32[]{:S(2)}, u32[]{:S(2)}) collective-permute-start(bf16[2,128,512]{2,1,0:T(8,128)(2,1)S(1)} %pad_maximum_fusion), channel_id=1, source_target_pairs={{0,1},{1,0},{2,3},{3,2},{4,5},{5,4},{6,7},{7,6},{8,9},{9,8},{10,11... | collective-permute-start | bytes 786440 | tf_op jit(solution)/shard_map/ppermute | solution.py:385
  17.1 1.1 %collective-permute-done.4 = bf16[2,128,512]{2,1,0:T(8,128)(2,1)S(1)} collective-permute-done((bf16[2,128,512]{2,1,0:T(8,128)(2,1)S(1)}, bf16[2,128,512]{2,1,0:T(8,128)(2,1)S(1)}, u32[]{:S(2)}, u32[]{:S(2)}) %collective-permute-start.4) | collective-permute-done | bytes 262176 | tf_op jit(solution)/shard_map/ppermute | solution.py:385
  18.3 0.0 copy-start
  18.3 0.8 %copy-done = bf16[2,256,512]{2,1,0:T(8,128)(2,1)} copy-done((bf16[2,256,512]{2,1,0:T(8,128)(2,1)}, bf16[2,256,512]{2,1,0:T(8,128)(2,1)S(1)}, u32[]{:S(2)}) %copy-start) | copy-done | bytes 524312
  19.1 7.7 %text.1 = (s32[256]{0:T(256)}, s32[256]{0:T(256)}, s32[2]{0:T(128)}, f32[32,1,128]{2,1,0:T(1,128)}, f32[32,1,128]{2,1,0:T(1,128)}, /*index=5*/f32[32,128,128]{2,1,0:T(8,128)}) custom-call(s32[4,8,9]{2,1,0:T(8,128)} %lists.1, s32[4,8]{1,0:T(4,128)} %lengths.1, bf16[1024,512]{1,0:T(8,128)(2,1)} %q_ref.1, bf16[2,256,512]{2,1,0:T(8,128)(2,1)} %copy-done), custom_call_target="tpu_custom_call" | custom-call | flops 1000000 | bytes 10000 | tf_op jit(solution)/shard_map/text/pallas_call | solution.py:420
  26.7 2.6 %collective-permute-start.7 = (bf16[1024,512]{1,0:T(8,128)(2,1)}, bf16[1024,512]{1,0:T(8,128)(2,1)}, u32[]{:S(2)}, u32[]{:S(2)}) collective-permute-start(bf16[1024,512]{1,0:T(8,128)(2,1)} %v_in.1), channel_id=1, source_target_pairs={{0,1},{1,2},{2,3},{3,4},{4,5},{5,6},{6,7},{7,8},{8,9},{9,10},{10,1... | collective-permute-start | bytes 3145736 | tf_op jit(solution)/shard_map/ppermute | solution.py:444
  29.3 1.9 %collective-permute-start.8 = (bf16[1024,512]{1,0:T(8,128)(2,1)}, bf16[1024,512]{1,0:T(8,128)(2,1)}, u32[]{:S(2)}, u32[]{:S(2)}) collective-permute-start(bf16[1024,512]{1,0:T(8,128)(2,1)} %v_in.1), channel_id=1, source_target_pairs={{1,0},{2,1},{3,2},{4,3},{5,4},{6,5},{7,6},{8,7},{9,8},{10,9},{11,1... | collective-permute-start | bytes 3145736 | tf_op jit(solution)/shard_map/ppermute | solution.py:445
  31.2 11.2 %own.1 = (f32[32,1,128]{2,1,0:T(1,128)}, f32[32,1,128]{2,1,0:T(1,128)}, f32[32,128,128]{2,1,0:T(8,128)}) custom-call(s32[256]{0:T(256)} %get-tuple-element.25.own_items, s32[2]{0:T(128)} %get-tuple-element.22.counts, bf16[1024,512]{1,0:T(8,128)(2,1)} %q_ref.1, bf16[1024,512]{1,0:T(8,128)(2,1)} %k_in.1, bf16[1024,512]{1,0:T(8,128)(2,1)} %v_in.1, ...), custom_call_target="tpu_custom_call" | custom-call | flops 1000000 | bytes 10000 | tf_op jit(solution)/shard_map/own/pallas_call | solution.py:447
  42.5 0.0 collective-permute-done.5.k_low
  42.5 7.1 %collective-permute-done.6.k_high = bf16[1024,512]{1,0:T(8,128)(2,1)} collective-permute-done((bf16[1024,512]{1,0:T(8,128)(2,1)}, bf16[1024,512]{1,0:T(8,128)(2,1)}, u32[]{:S(2)}, u32[]{:S(2)}) %collective-permute-start.6) | collective-permute-done | bytes 1048608 | tf_op jit(solution)/shard_map/ppermute | solution.py:412
  49.6 10.8 %middle.1 = (f32[1024,512]{1,0:T(8,128)}, bf16[256,128,128]{2,1,0:T(8,128)(2,1)}) custom-call(s32[256]{0:T(256)} %get-tuple-element.21.far_items, s32[2]{0:T(128)} %get-tuple-element.22.counts, bf16[1024,512]{1,0:T(8,128)(2,1)} %q_ref.1, bf16[1024,512]{1,0:T(8,128)(2,1)} %collective-permute-done.5.k_low, bf16[1024,512]{1,0:T(8,128)(2,1)} %collective-permute-done.6.k_high, ...), custom_call_target="tpu_custom_call" | custom-call | flops 1000000 | bytes 10000 | tf_op jit(solution)/shard_map/middle/pallas_call | solution.py:479
  60.4 0.0 collective-permute-done.7.v_low
  60.4 0.4 collective-permute-done.8.v_high
  60.8 6.8 %last.1 = bf16[1024,512]{1,0:T(8,128)(2,1)} custom-call(s32[256]{0:T(256)} %get-tuple-element.21.far_items, s32[2]{0:T(128)} %get-tuple-element.22.counts, f32[1024,512]{1,0:T(8,128)} %get-tuple-element.32.near, bf16[256,128,128]{2,1,0:T(8,128)(2,1)} %get-tuple-element.33.weights, bf16[1024,512]{1,0:T(8,128)(2,1)} %collective-permute-done.7.v_low, ...), custom_call_target="tpu_custom_call" | custom-call | flops 1000000000 | bytes 9000000 | tf_op jit(solution)/shard_map/last/pallas_call | solution.py:506
  (6 shorter events, 0.1 us)
Async XLA Ops:
  0.7 2.8 %collective-permute-start = (bf16[2,16,512]{2,1,0:T(8,128)(2,1)S(1)}, bf16[2,16,512]{2,1,0:T(8,128)(2,1)S(1)}, u32[]{:S(2)}, u32[]{:S(2)}) collective-permute-start(bf16[2,16,512]{2,1,0:T(8,128)(2,1)S(1)} %pad_maximum_fusion.2), channel_id=1, source_target_pairs={{0,2},{1,3},{2,0},{3,1},{4,6},{5,7},{6,4},{7,5},{8,10},{9,11},{10,... | collective-permute-start | bytes 98312 | tf_op jit(solution)/shard_map/ppermute | solution.py:385
  4.2 11.2 %collective-permute-start.1 = (bf16[2,32,512]{2,1,0:T(8,128)(2,1)S(1)}, bf16[2,32,512]{2,1,0:T(8,128)(2,1)S(1)}, u32[]{:S(2)}, u32[]{:S(2)}) collective-permute-start(bf16[2,32,512]{2,1,0:T(8,128)(2,1)S(1)} %pad_maximum_fusion.1), channel_id=1, source_target_pairs={{0,4},{1,5},{2,6},{3,7},{4,0},{5,1},{6,2},{7,3},{8,12},{9,13},{10,... | collective-permute-start | bytes 196616 | tf_op jit(solution)/shard_map/ppermute | solution.py:385
  4.4 11.0 %collective-permute-start.2 = (bf16[2,32,512]{2,1,0:T(8,128)(2,1)S(1)}, bf16[2,32,512]{2,1,0:T(8,128)(2,1)S(1)}, u32[]{:S(2)}, u32[]{:S(2)}) collective-permute-start(bf16[2,32,512]{2,1,0:T(8,128)(2,1)S(1)} %pad_maximum_fusion.1), channel_id=1, source_target_pairs={{0,8},{1,9},{2,10},{3,11},{4,12},{5,13},{6,14},{7,15},{8,0},{9,1},... | collective-permute-start | bytes 196616 | tf_op jit(solution)/shard_map/ppermute | solution.py:385
  4.4 11.0 %collective-permute-start.3 = (bf16[2,32,512]{2,1,0:T(8,128)(2,1)S(1)}, bf16[2,32,512]{2,1,0:T(8,128)(2,1)S(1)}, u32[]{:S(2)}, u32[]{:S(2)}) collective-permute-start(bf16[2,32,512]{2,1,0:T(8,128)(2,1)S(1)} %pad_maximum_fusion.1), channel_id=1, source_target_pairs={{0,12},{1,13},{2,14},{3,15},{4,8},{5,9},{6,10},{7,11},{8,4},{9,5},... | collective-permute-start | bytes 196616 | tf_op jit(solution)/shard_map/ppermute | solution.py:385
  7.8 34.7 %collective-permute-start.5 = (bf16[1024,512]{1,0:T(8,128)(2,1)}, bf16[1024,512]{1,0:T(8,128)(2,1)}, u32[]{:S(2)}, u32[]{:S(2)}) collective-permute-start(bf16[1024,512]{1,0:T(8,128)(2,1)} %k_in.1), channel_id=1, source_target_pairs={{0,1},{1,2},{2,3},{3,4},{4,5},{5,6},{6,7},{7,8},{8,9},{9,10},{10,1... | collective-permute-start | bytes 3145736 | tf_op jit(solution)/shard_map/ppermute | solution.py:411
  13.5 36.1 %collective-permute-start.6 = (bf16[1024,512]{1,0:T(8,128)(2,1)}, bf16[1024,512]{1,0:T(8,128)(2,1)}, u32[]{:S(2)}, u32[]{:S(2)}) collective-permute-start(bf16[1024,512]{1,0:T(8,128)(2,1)} %k_in.1), channel_id=1, source_target_pairs={{1,0},{2,1},{3,2},{4,3},{5,4},{6,5},{7,6},{8,7},{9,8},{10,9},{11,1... | collective-permute-start | bytes 3145736 | tf_op jit(solution)/shard_map/ppermute | solution.py:412
  15.5 2.8 %collective-permute-start.4 = (bf16[2,128,512]{2,1,0:T(8,128)(2,1)S(1)}, bf16[2,128,512]{2,1,0:T(8,128)(2,1)S(1)}, u32[]{:S(2)}, u32[]{:S(2)}) collective-permute-start(bf16[2,128,512]{2,1,0:T(8,128)(2,1)S(1)} %pad_maximum_fusion), channel_id=1, source_target_pairs={{0,1},{1,0},{2,3},{3,2},{4,5},{5,4},{6,7},{7,6},{8,9},{9,8},{10,11... | collective-permute-start | bytes 786440 | tf_op jit(solution)/shard_map/ppermute | solution.py:385
  18.3 0.8 %copy-start = (bf16[2,256,512]{2,1,0:T(8,128)(2,1)}, bf16[2,256,512]{2,1,0:T(8,128)(2,1)S(1)}, u32[]{:S(2)}) copy-start(bf16[2,256,512]{2,1,0:T(8,128)(2,1)S(1)} %constant_dynamic-update-slice_fusion.text_in) | copy-start | bytes 1572868
  26.7 33.7 %collective-permute-start.7 = (bf16[1024,512]{1,0:T(8,128)(2,1)}, bf16[1024,512]{1,0:T(8,128)(2,1)}, u32[]{:S(2)}, u32[]{:S(2)}) collective-permute-start(bf16[1024,512]{1,0:T(8,128)(2,1)} %v_in.1), channel_id=1, source_target_pairs={{0,1},{1,2},{2,3},{3,4},{4,5},{5,6},{6,7},{7,8},{8,9},{9,10},{10,1... | collective-permute-start | bytes 3145736 | tf_op jit(solution)/shard_map/ppermute | solution.py:444
  29.3 31.5 %collective-permute-start.8 = (bf16[1024,512]{1,0:T(8,128)(2,1)}, bf16[1024,512]{1,0:T(8,128)(2,1)}, u32[]{:S(2)}, u32[]{:S(2)}) collective-permute-start(bf16[1024,512]{1,0:T(8,128)(2,1)} %v_in.1), channel_id=1, source_target_pairs={{1,0},{2,1},{3,2},{4,3},{5,4},{6,5},{7,6},{8,7},{9,8},{10,9},{11,1... | collective-permute-start | bytes 3145736 | tf_op jit(solution)/shard_map/ppermute | solution.py:445

commit v2 on v1

--- a/solution.py
+++ b/solution.py
@@ -57,7 +57,7 @@
     lengths,
     q_in,
     text_in,
-    own_items,
+    near_items,
     far_items,
     counts,
     tops,
@@ -75,33 +75,38 @@
     for copy in copies:
         copy.start()
     base = lists[0, 0, 0]
+    odd = (base // blocks_dev) % 2 == 1
 
     def plan_unit(unit, carry):
         head = unit // blocks_dev
         local = unit % blocks_dev
 
         def plan_entry(entry, carry):
-            own, far = carry
+            near, far = carry
             block = lists[head, local, entry] - base
-            code = unit * CODE
-            is_own = jnp.logical_and(block >= 0, block < blocks_dev)
-
-            @pl.when(is_own)
+            is_low = block < 0
+            is_high = block >= blocks_dev
+            is_outer = jnp.where(odd, is_high, is_low)
+            is_inner = jnp.where(odd, is_low, is_high)
+            shift = jnp.where(is_low, blocks_dev, jnp.where(is_high, -blocks_dev, 0))
+            code = unit * CODE + block + shift
+
+            @pl.when(is_outer)
             def _():
-                own_items[own] = code + block
-
-            @pl.when(jnp.logical_not(is_own))
+                far_items[far] = code
+
+            @pl.when(jnp.logical_not(is_outer))
             def _():
-                far_items[far] = code + jnp.where(block < 0, block + blocks_dev, block)
-
-            mine = is_own.astype(jnp.int32)
-            return own + mine, far + 1 - mine
+                near_items[near] = code + jnp.where(is_inner, blocks_dev, 0)
+
+            outer = is_outer.astype(jnp.int32)
+            return near + 1 - outer, far + outer
 
         return lax.fori_loop(0, lengths[head, local], plan_entry, carry)
 
     zero = jnp.int32(0)
-    own, far = lax.fori_loop(0, HEADS * blocks_dev, plan_unit, (zero, zero))
-    counts[0] = own
+    near, far = lax.fori_loop(0, HEADS * blocks_dev, plan_unit, (zero, zero))
+    counts[0] = near
     counts[1] = far
     for copy in copies:
         copy.wait()
@@ -139,13 +144,15 @@
     lax.fori_loop(0, HEADS, sums_head, 0)
 
 
-def own_kernel(
+def near_kernel(
     blocks_dev,
-    own_items,
+    near_items,
     counts,
     q_in,
     k_in,
     v_in,
+    k_inner,
+    v_inner,
     sums_in,
     text_tops,
     text_totals,
@@ -160,13 +167,23 @@
     weights_all,
     sems,
 ):
+    tokens = k_in.shape[0]
+    first, second = pl.ds(0, tokens), pl.ds(tokens, tokens)
+    moves = (
+        (q_in, q_ref),
+        (k_in, k_ref.at[first]),
+        (k_inner, k_ref.at[second]),
+        (v_in, v_ref.at[first]),
+        (v_inner, v_ref.at[second]),
+        (sums_in, sums),
+    )
     copies = [
         pltpu.make_async_copy(source, target, sems.at[index])
-        for index, (source, target) in enumerate(((q_in, q_ref), (k_in, k_ref), (v_in, v_ref), (sums_in, sums)))
+        for index, (source, target) in enumerate(moves)
     ]
     for copy in copies:
         copy.start()
-    own = counts[0]
+    count = counts[0]
 
     def turn(block, carry):
         for head in range(HEADS):
@@ -175,8 +192,8 @@
         return carry
 
     tops[...] = text_tops[...]
-    copies[0].wait()
-    copies[1].wait()
+    for copy in copies[:3]:
+        copy.wait()
 
     def top_body(slots):
         found = []
@@ -189,10 +206,10 @@
         for unit, top in found:
             tops[unit] = jnp.maximum(tops[unit], top)
 
-    for_groups(own, own_items, blocks_dev, top_body)
+    for_groups(count, near_items, blocks_dev, top_body)
     factor = jnp.exp2((text_tops[...] - tops[...]) * EXP2_SCALE)
     totals[...] = text_totals[...] * factor
-    copies[3].wait()
+    copies[5].wait()
     sums[...] = sums[...] * factor
 
     def weights_body(slots):
@@ -205,7 +222,7 @@
         for unit, total in found:
             totals[unit] += total
 
-    for_groups(own, own_items, blocks_dev, weights_body)
+    for_groups(count, near_items, blocks_dev, weights_body)
 
     def sum_body(slots):
         found = []
@@ -219,9 +236,10 @@
         for unit, summed in found:
             sums[unit] += summed
 
-    copies[2].wait()
-    lax.fori_loop(0, blocks_dev, turn, 0)
-    for_groups(own, own_items, blocks_dev, sum_body)
+    copies[3].wait()
+    copies[4].wait()
+    lax.fori_loop(0, 2 * blocks_dev, turn, 0)
+    for_groups(count, near_items, blocks_dev, sum_body)
 
 
 def middle_kernel(
@@ -229,14 +247,12 @@
     far_items,
     counts,
     q_ref,
-    k_low,
-    k_high,
+    k_far,
     near_tops,
     near_totals,
     sums,
     near_out,
     weights_out,
-    k_far,
     tops,
     totals,
     levels,
@@ -244,20 +260,10 @@
     item_totals,
     scores_all,
     weights_all,
-    sems,
     out_sems,
 ):
-    tokens = k_low.shape[0]
-    copies = [
-        pltpu.make_async_copy(k_low, k_far.at[pl.ds(0, tokens)], sems.at[0]),
-        pltpu.make_async_copy(k_high, k_far.at[pl.ds(tokens, tokens)], sems.at[1]),
-    ]
-    for copy in copies:
-        copy.start()
     tops[...] = near_tops[...]
     totals[...] = near_totals[...]
-    for copy in copies:
-        copy.wait()
     count = counts[1]
 
     def total_body(slots):
@@ -327,8 +333,7 @@
     counts,
     near,
     weights,
-    v_low,
-    v_high,
+    v_outer,
     out_ref,
     v_far,
     total_rows,
@@ -336,7 +341,6 @@
     sems,
     weight_sems,
 ):
-    tokens = v_low.shape[0]
     count = counts[1]
     groups = (count + GROUP - 1) // GROUP
 
@@ -345,9 +349,8 @@
         return pltpu.make_async_copy(weights.at[part], weights_all.at[part], weight_sems.at[group])
 
     copies = [
-        pltpu.make_async_copy(v_low, v_far.at[pl.ds(0, tokens)], sems.at[0]),
-        pltpu.make_async_copy(v_high, v_far.at[pl.ds(tokens, tokens)], sems.at[1]),
-        pltpu.make_async_copy(near, total_rows, sems.at[2]),
+        pltpu.make_async_copy(v_outer, v_far, sems.at[0]),
+        pltpu.make_async_copy(near, total_rows, sems.at[1]),
     ]
     for copy in copies:
         copy.start()
@@ -394,8 +397,9 @@
     assert blocks_dev == REACH and 2 * blocks_dev <= CODE and count & (count - 1) == 0
     units = HEADS * blocks_dev
     longest = block_lists.shape[2]
-    forward = [(i, i + 1) for i in range(count - 1)]
-    backward = [(target, source) for source, target in forward]
+    inner = [(i, i ^ 1) for i in range(count)]
+    outer = [(i, i + 1) for i in range(1, count - 1, 2)]
+    outer += [(target, source) for source, target in outer]
 
     smem = pl.BlockSpec(memory_space=pltpu.SMEM)
     vmem = pl.BlockSpec(memory_space=pltpu.VMEM)
@@ -403,13 +407,16 @@
     stat = (units, 1, BLOCK)
     squares = (units, HEAD_DIM, BLOCK)
     room = -(-units * (longest - 1) // GROUP) * GROUP
+    near_room = -(-units * longest // GROUP) * GROUP
     weights_shape = (room, BLOCK, BLOCK)
+    near_shape = (near_room, BLOCK, BLOCK)
     params = pltpu.CompilerParams(vmem_limit_bytes=VMEM_BYTES)
 
     text = text_step(jnp.stack([text_keys, text_values], 0), (2,))
     keys, text = lax.optimization_barrier((video_keys, text))
-    k_low = lax.ppermute(keys, "seq", forward)
-    k_high = lax.ppermute(keys, "seq", backward)
+    k_outer = lax.ppermute(keys, "seq", outer)
+    k_inner = lax.ppermute(video_keys, "seq", inner)
+    v_inner = lax.ppermute(video_values, "seq", inner)
     text = text_step(text, (4, 8, 12) if count >= 16 else (4,) if count == 8 else ())
     distance = 16
     while distance < count:
@@ -417,10 +424,10 @@
         distance *= 2
     text = text_step(text, (1,))
 
-    own_items, far_items, counts, text_tops, text_totals, text_sums = pl.pallas_call(
+    near_items, far_items, counts, text_tops, text_totals, text_sums = pl.pallas_call(
         functools.partial(text_kernel, blocks_dev),
         out_shape=(
-            jax.ShapeDtypeStruct((units * blocks_dev,), jnp.int32),
+            jax.ShapeDtypeStruct((near_room,), jnp.int32),
             jax.ShapeDtypeStruct((room,), jnp.int32),
             jax.ShapeDtypeStruct((2,), jnp.int32),
             jax.ShapeDtypeStruct(stat, jnp.float32),
@@ -440,37 +447,38 @@
         name="text",
     )(block_lists, list_lengths, queries, text)
 
-    values, own_items = lax.optimization_barrier((video_values, own_items))
-    v_low = lax.ppermute(values, "seq", forward)
-    v_high = lax.ppermute(values, "seq", backward)
+    values, near_items = lax.optimization_barrier((video_values, near_items))
+    v_outer = lax.ppermute(values, "seq", outer)
 
     tops, totals, sums = pl.pallas_call(
-        functools.partial(own_kernel, blocks_dev),
+        functools.partial(near_kernel, blocks_dev),
         out_shape=(
             jax.ShapeDtypeStruct(stat, jnp.float32),
             jax.ShapeDtypeStruct(stat, jnp.float32),
             jax.ShapeDtypeStruct(squares, jnp.float32),
         ),
-        in_specs=[smem, smem] + [anywhere] * 4 + [vmem] * 2,
+        in_specs=[smem, smem] + [anywhere] * 6 + [vmem] * 2,
         out_specs=(vmem, vmem, vmem),
         scratch_shapes=[
             pltpu.VMEM((tokens, columns), jnp.bfloat16),
-            pltpu.VMEM((tokens, columns), jnp.bfloat16),
-            pltpu.VMEM((tokens, columns), jnp.bfloat16),
-            pltpu.VMEM((columns, tokens), jnp.bfloat16),
-            pltpu.VMEM((units * blocks_dev, BLOCK, BLOCK), jnp.float32),
-            pltpu.VMEM((units * blocks_dev, BLOCK, BLOCK), jnp.bfloat16),
-            pltpu.SemaphoreType.DMA((4,)),
+            pltpu.VMEM((2 * tokens, columns), jnp.bfloat16),
+            pltpu.VMEM((2 * tokens, columns), jnp.bfloat16),
+            pltpu.VMEM((columns, 2 * tokens), jnp.bfloat16),
+            pltpu.VMEM(near_shape, jnp.float32),
+            pltpu.VMEM(near_shape, jnp.bfloat16),
+            pltpu.SemaphoreType.DMA((6,)),
         ],
         compiler_params=params,
         cost_estimate=pl.CostEstimate(flops=1_000_000, bytes_accessed=10_000, transcendentals=0),
         name="own",
     )(
-        own_items,
+        near_items,
         counts,
         queries,
         video_keys,
         video_values,
+        k_inner,
+        v_inner,
         text_sums,
         text_tops,
         text_totals,
@@ -482,10 +490,9 @@
             jax.ShapeDtypeStruct((tokens, columns), jnp.float32),
             jax.ShapeDtypeStruct(weights_shape, jnp.bfloat16),
         ),
-        in_specs=[smem, smem, vmem, anywhere, anywhere] + [vmem] * 3,
+        in_specs=[smem, smem] + [vmem] * 5,
         out_specs=(vmem, anywhere),
         scratch_shapes=[
-            pltpu.VMEM((2 * tokens, columns), jnp.bfloat16),
             pltpu.VMEM(stat, jnp.float32),
             pltpu.VMEM(stat, jnp.float32),
             pltpu.VMEM(stat, jnp.float32),
@@ -493,7 +500,6 @@
             pltpu.VMEM((room, 1, BLOCK), jnp.float32),
             pltpu.VMEM(weights_shape, jnp.float32),
             pltpu.VMEM(weights_shape, jnp.bfloat16),
-            pltpu.SemaphoreType.DMA((2,)),
             pltpu.SemaphoreType.DMA((room // GROUP,)),
         ],
         compiler_params=params,
@@ -501,18 +507,18 @@
             flops=1_000_000, bytes_accessed=10_000, transcendentals=0
         ),
         name="middle",
-    )(far_items, counts, queries, k_low, k_high, tops, totals, sums)
+    )(far_items, counts, queries, k_outer, tops, totals, sums)
 
     return pl.pallas_call(
         functools.partial(last_kernel, blocks_dev),
         out_shape=jax.ShapeDtypeStruct((tokens, columns), jnp.bfloat16),
-        in_specs=[smem, smem] + [anywhere] * 4,
+        in_specs=[smem, smem] + [anywhere] * 3,
         out_specs=vmem,
         scratch_shapes=[
-            pltpu.VMEM((2 * tokens, columns), jnp.bfloat16),
+            pltpu.VMEM((tokens, columns), jnp.bfloat16),
             pltpu.VMEM((tokens, columns), jnp.float32),
             pltpu.VMEM(weights_shape, jnp.bfloat16),
-            pltpu.SemaphoreType.DMA((3,)),
+            pltpu.SemaphoreType.DMA((2,)),
             pltpu.SemaphoreType.DMA((room // GROUP,)),
         ],
         compiler_params=params,
@@ -520,7 +526,7 @@
             flops=1_000_000_000, bytes_accessed=9_000_000, transcendentals=0
         ),
         name="last",
-    )(far_items, counts, near, weights, v_low, v_high)
+    )(far_items, counts, near, weights, v_outer)
 
 
 def solution(mesh):

time: 68.2 us -> 66.6 us (0.977)
  the two profiles are of different devices: /device:TPU:25 before, /device:TPU:9 now
where the time goes in v2:
time: 66.6 us; the launch traced here: 65.9 us
  Pallas kernels  35.9 us (54%)
  starting transfers between devices  13.8 us (21%)
  waiting for transfers between devices  13.7 us (21%)
  other arithmetic  1.5 us (2%)
  local copies, waits for them, and re-layouts  0.83 us (1%)
    pallas_call x1, Pallas kernels, on_device(): pl.pallas_call(functools.partial(near_kernel, blocks_dev), out_shape=(jax...  14.5 us
    pallas_call x1, Pallas kernels, on_device(): pl.pallas_call(functools.partial(text_kernel, blocks_dev), out_shape=(jax...  8.18 us
    pallas_call x1, Pallas kernels, on_device(): pl.pallas_call(functools.partial(middle_kernel, blocks_dev), out_shape=(j...  7.78 us
    ppermute x1, waiting for transfers between devices, on_device(): k_outer = lax.ppermute(keys, 'seq', outer)  7.76 us
    ppermute x1, starting transfers between devices, on_device(): k_outer = lax.ppermute(keys, 'seq', outer)  6.65 us
    pallas_call x1, Pallas kernels, on_device(): pl.pallas_call(functools.partial(last_kernel, blocks_dev), out_shape=jax....  5.36 us
    ppermute x5, starting transfers between devices, text_step(): lax.ppermute(text, 'seq', [(i, i ^ distance) for i in range(count)])  3.93 us
    ppermute x1, waiting for transfers between devices, on_device(): v_outer = lax.ppermute(values, 'seq', outer)  3.44 us
  transfers between devices with their start and end apart: 9, of which 5 were waited for; matrix products, arithmetic and copies ran while one was open for 1% of the time, Pallas kernels for 46%

profile of v2, /device:TPU:9, one launch (start us, length us, event | category | flops | bytes accessed | tf_op | source)
XLA Modules:
  0.0 65.9 jit_solution(9046759800573924587)
XLA Ops:
  0.0 0.7 %pad_maximum_fusion.2 = bf16[2,16,512]{2,1,0:T(8,128)(2,1)S(1)} fusion(bf16[1,16,512]{2,1,0:T(8,128)(2,1)} %bitcast.2, bf16[1,16,512]{2,1,0:T(8,128)(2,1)} %bitcast.4), kind=kLoop, calls=%fused_computation.2 | loop fusion | flops 16384 | bytes 65536 | tf_op jit(solution)/shard_map/stack | solution.py:415
  0.7 1.2 %collective-permute-start = (bf16[2,16,512]{2,1,0:T(8,128)(2,1)S(1)}, bf16[2,16,512]{2,1,0:T(8,128)(2,1)S(1)}, u32[]{:S(2)}, u32[]{:S(2)}) collective-permute-start(bf16[2,16,512]{2,1,0:T(8,128)(2,1)S(1)} %pad_maximum_fusion.2), channel_id=1, source_target_pairs={{0,2},{1,3},{2,0},{3,1},{4,6},{5,7},{6,4},{7,5},{8,10},{9,11},{10,... | collective-permute-start | bytes 98312 | tf_op jit(solution)/shard_map/ppermute | solution.py:388
  2.0 1.0 %collective-permute-start.6 = (bf16[1024,512]{1,0:T(8,128)(2,1)}, bf16[1024,512]{1,0:T(8,128)(2,1)}, u32[]{:S(2)}, u32[]{:S(2)}) collective-permute-start(bf16[1024,512]{1,0:T(8,128)(2,1)} %k_in.1), channel_id=1, source_target_pairs={{0,1},{1,0},{2,3},{3,2},{4,5},{5,4},{6,7},{7,6},{8,9},{9,8},{10,11... | collective-permute-start | bytes 3145736 | tf_op jit(solution)/shard_map/ppermute | solution.py:418
  2.9 0.0 collective-permute-start.7
  2.9 0.6 collective-permute-done
  3.5 0.7 %pad_maximum_fusion.1 = bf16[2,32,512]{2,1,0:T(8,128)(2,1)S(1)} fusion(bf16[2,16,512]{2,1,0:T(8,128)(2,1)S(1)} %collective-permute-done, bf16[1,16,512]{2,1,0:T(8,128)(2,1)} %bitcast.3, bf16[1,16,512]{2,1,0:T(8,128)(2,1)} %bitcast.5), kind=kLoop, calls=%fused_computation.1 | loop fusion | flops 196608 | bytes 131072 | tf_op jit(solution)/shard_map/concatenate | solution.py:389
  4.2 0.0 collective-permute-start.1
  4.2 2.5 %collective-permute-start.2 = (bf16[2,32,512]{2,1,0:T(8,128)(2,1)S(1)}, bf16[2,32,512]{2,1,0:T(8,128)(2,1)S(1)}, u32[]{:S(2)}, u32[]{:S(2)}) collective-permute-start(bf16[2,32,512]{2,1,0:T(8,128)(2,1)S(1)} %pad_maximum_fusion.1), channel_id=1, source_target_pairs={{0,8},{1,9},{2,10},{3,11},{4,12},{5,13},{6,14},{7,15},{8,0},{9,1},... | collective-permute-start | bytes 196616 | tf_op jit(solution)/shard_map/ppermute | solution.py:388
  6.7 0.2 collective-permute-start.3
  6.9 0.5 collective-permute-done.1
  7.4 6.6 %collective-permute-start.5 = (bf16[1024,512]{1,0:T(8,128)(2,1)}, bf16[1024,512]{1,0:T(8,128)(2,1)}, u32[]{:S(2)}, u32[]{:S(2)}) collective-permute-start(bf16[1024,512]{1,0:T(8,128)(2,1)} %k_in.1), channel_id=1, source_target_pairs={{1,2},{3,4},{5,6},{7,8},{9,10},{11,12},{13,14},{2,1},{4,3},{6,5},{... | collective-permute-start | bytes 3145736 | tf_op jit(solution)/shard_map/ppermute | solution.py:417
  14.0 0.0 collective-permute-done.2
  14.0 0.0 collective-permute-done.3
  14.1 0.1 collective-permute-start.4
  14.2 1.5 %collective-permute-done.4 = bf16[2,128,512]{2,1,0:T(8,128)(2,1)S(1)} collective-permute-done((bf16[2,128,512]{2,1,0:T(8,128)(2,1)S(1)}, bf16[2,128,512]{2,1,0:T(8,128)(2,1)S(1)}, u32[]{:S(2)}, u32[]{:S(2)}) %collective-permute-start.4) | collective-permute-done | bytes 262176 | tf_op jit(solution)/shard_map/ppermute | solution.py:388
  15.7 0.0 copy-start
  15.7 0.8 %copy-done = bf16[2,256,512]{2,1,0:T(8,128)(2,1)} copy-done((bf16[2,256,512]{2,1,0:T(8,128)(2,1)}, bf16[2,256,512]{2,1,0:T(8,128)(2,1)S(1)}, u32[]{:S(2)}) %copy-start) | copy-done | bytes 524312
  16.5 8.2 %text.1 = (s32[288]{0:T(512)}, s32[256]{0:T(256)}, s32[2]{0:T(128)}, f32[32,1,128]{2,1,0:T(1,128)}, f32[32,1,128]{2,1,0:T(1,128)}, /*index=5*/f32[32,128,128]{2,1,0:T(8,128)}) custom-call(s32[4,8,9]{2,1,0:T(8,128)} %lists.1, s32[4,8]{1,0:T(4,128)} %lengths.1, bf16[1024,512]{1,0:T(8,128)(2,1)} %q_ref.1, bf16[2,256,512]{2,1,0:T(8,128)(2,1)} %copy-done), custom_call_target="tpu_custom_call" | custom-call | flops 1000000 | bytes 10000 | tf_op jit(solution)/shard_map/text/pallas_call | solution.py:427
  24.7 2.3 %collective-permute-start.8 = (bf16[1024,512]{1,0:T(8,128)(2,1)}, bf16[1024,512]{1,0:T(8,128)(2,1)}, u32[]{:S(2)}, u32[]{:S(2)}) collective-permute-start(bf16[1024,512]{1,0:T(8,128)(2,1)} %v_in.1), channel_id=1, source_target_pairs={{1,2},{3,4},{5,6},{7,8},{9,10},{11,12},{13,14},{2,1},{4,3},{6,5},{... | collective-permute-start | bytes 3145736 | tf_op jit(solution)/shard_map/ppermute | solution.py:451
  26.9 0.0 collective-permute-done.6.k_inner
  27.0 0.0 collective-permute-done.7.v_inner
  27.0 14.5 %own.1 = (f32[32,1,128]{2,1,0:T(1,128)}, f32[32,1,128]{2,1,0:T(1,128)}, f32[32,128,128]{2,1,0:T(8,128)}) custom-call(s32[288]{0:T(512)} %get-tuple-element.25.near_items, s32[2]{0:T(128)} %get-tuple-element.22.counts, bf16[1024,512]{1,0:T(8,128)(2,1)} %q_ref.1, bf16[1024,512]{1,0:T(8,128)(2,1)} %k_in.1, bf16[1024,512]{1,0:T(8,128)(2,1)} %v_in.1, ...), custom_call_target="tpu_custom_call" | custom-call | flops 1000000 | bytes 10000 | tf_op jit(solution)/shard_map/own/pallas_call | solution.py:453
  41.5 7.8 %collective-permute-done.5.k_far = bf16[1024,512]{1,0:T(8,128)(2,1)} collective-permute-done((bf16[1024,512]{1,0:T(8,128)(2,1)}, bf16[1024,512]{1,0:T(8,128)(2,1)}, u32[]{:S(2)}, u32[]{:S(2)}) %collective-permute-start.5) | collective-permute-done | bytes 1048608 | tf_op jit(solution)/shard_map/ppermute | solution.py:417
  49.3 7.8 %middle.1 = (f32[1024,512]{1,0:T(8,128)}, bf16[256,128,128]{2,1,0:T(8,128)(2,1)}) custom-call(s32[256]{0:T(256)} %get-tuple-element.21.far_items, s32[2]{0:T(128)} %get-tuple-element.22.counts, bf16[1024,512]{1,0:T(8,128)(2,1)} %q_ref.1, bf16[1024,512]{1,0:T(8,128)(2,1)} %collective-permute-done.5.k_far, f32[32,1,128]{2,1,0:T(1,128)} %get-tuple-element.29.near_tops, ...), custom_call_target="tpu_custom_call" | custom-call | flops 1000000 | bytes 10000 | tf_op jit(solution)/shard_map/middle/pallas_call | solution.py:487
  57.1 3.4 %collective-permute-done.8.v_outer = bf16[1024,512]{1,0:T(8,128)(2,1)} collective-permute-done((bf16[1024,512]{1,0:T(8,128)(2,1)}, bf16[1024,512]{1,0:T(8,128)(2,1)}, u32[]{:S(2)}, u32[]{:S(2)}) %collective-permute-start.8) | collective-permute-done | bytes 1048608 | tf_op jit(solution)/shard_map/ppermute | solution.py:451
  60.5 5.4 %last.1 = bf16[1024,512]{1,0:T(8,128)(2,1)} custom-call(s32[256]{0:T(256)} %get-tuple-element.21.far_items, s32[2]{0:T(128)} %get-tuple-element.22.counts, f32[1024,512]{1,0:T(8,128)} %get-tuple-element.32.near, bf16[256,128,128]{2,1,0:T(8,128)(2,1)} %get-tuple-element.33.weights, bf16[1024,512]{1,0:T(8,128)(2,1)} %collective-permute-done.8.v_outer), custom_call_target="tpu_custom_call" | custom-call | flops 1000000000 | bytes 9000000 | tf_op jit(solution)/shard_map/last/pallas_call | solution.py:512
  (6 shorter events, 0.1 us)
Async XLA Ops:
  0.7 2.8 %collective-permute-start = (bf16[2,16,512]{2,1,0:T(8,128)(2,1)S(1)}, bf16[2,16,512]{2,1,0:T(8,128)(2,1)S(1)}, u32[]{:S(2)}, u32[]{:S(2)}) collective-permute-start(bf16[2,16,512]{2,1,0:T(8,128)(2,1)S(1)} %pad_maximum_fusion.2), channel_id=1, source_target_pairs={{0,2},{1,3},{2,0},{3,1},{4,6},{5,7},{6,4},{7,5},{8,10},{9,11},{10,... | collective-permute-start | bytes 98312 | tf_op jit(solution)/shard_map/ppermute | solution.py:388
  2.0 25.0 %collective-permute-start.6 = (bf16[1024,512]{1,0:T(8,128)(2,1)}, bf16[1024,512]{1,0:T(8,128)(2,1)}, u32[]{:S(2)}, u32[]{:S(2)}) collective-permute-start(bf16[1024,512]{1,0:T(8,128)(2,1)} %k_in.1), channel_id=1, source_target_pairs={{0,1},{1,0},{2,3},{3,2},{4,5},{5,4},{6,7},{7,6},{8,9},{9,8},{10,11... | collective-permute-start | bytes 3145736 | tf_op jit(solution)/shard_map/ppermute | solution.py:418
  2.9 24.1 %collective-permute-start.7 = (bf16[1024,512]{1,0:T(8,128)(2,1)}, bf16[1024,512]{1,0:T(8,128)(2,1)}, u32[]{:S(2)}, u32[]{:S(2)}) collective-permute-start(bf16[1024,512]{1,0:T(8,128)(2,1)} %v_in.1), channel_id=1, source_target_pairs={{0,1},{1,0},{2,3},{3,2},{4,5},{5,4},{6,7},{7,6},{8,9},{9,8},{10,11... | collective-permute-start | bytes 3145736 | tf_op jit(solution)/shard_map/ppermute | solution.py:419
  4.2 3.1 %collective-permute-start.1 = (bf16[2,32,512]{2,1,0:T(8,128)(2,1)S(1)}, bf16[2,32,512]{2,1,0:T(8,128)(2,1)S(1)}, u32[]{:S(2)}, u32[]{:S(2)}) collective-permute-start(bf16[2,32,512]{2,1,0:T(8,128)(2,1)S(1)} %pad_maximum_fusion.1), channel_id=1, source_target_pairs={{0,4},{1,5},{2,6},{3,7},{4,0},{5,1},{6,2},{7,3},{8,12},{9,13},{10,... | collective-permute-start | bytes 196616 | tf_op jit(solution)/shard_map/ppermute | solution.py:388
  4.2 9.8 %collective-permute-start.2 = (bf16[2,32,512]{2,1,0:T(8,128)(2,1)S(1)}, bf16[2,32,512]{2,1,0:T(8,128)(2,1)S(1)}, u32[]{:S(2)}, u32[]{:S(2)}) collective-permute-start(bf16[2,32,512]{2,1,0:T(8,128)(2,1)S(1)} %pad_maximum_fusion.1), channel_id=1, source_target_pairs={{0,8},{1,9},{2,10},{3,11},{4,12},{5,13},{6,14},{7,15},{8,0},{9,1},... | collective-permute-start | bytes 196616 | tf_op jit(solution)/shard_map/ppermute | solution.py:388
  6.7 7.3 %collective-permute-start.3 = (bf16[2,32,512]{2,1,0:T(8,128)(2,1)S(1)}, bf16[2,32,512]{2,1,0:T(8,128)(2,1)S(1)}, u32[]{:S(2)}, u32[]{:S(2)}) collective-permute-start(bf16[2,32,512]{2,1,0:T(8,128)(2,1)S(1)} %pad_maximum_fusion.1), channel_id=1, source_target_pairs={{0,12},{1,13},{2,14},{3,15},{4,8},{5,9},{6,10},{7,11},{8,4},{9,5},... | collective-permute-start | bytes 196616 | tf_op jit(solution)/shard_map/ppermute | solution.py:388
  7.4 41.9 %collective-permute-start.5 = (bf16[1024,512]{1,0:T(8,128)(2,1)}, bf16[1024,512]{1,0:T(8,128)(2,1)}, u32[]{:S(2)}, u32[]{:S(2)}) collective-permute-start(bf16[1024,512]{1,0:T(8,128)(2,1)} %k_in.1), channel_id=1, source_target_pairs={{1,2},{3,4},{5,6},{7,8},{9,10},{11,12},{13,14},{2,1},{4,3},{6,5},{... | collective-permute-start | bytes 3145736 | tf_op jit(solution)/shard_map/ppermute | solution.py:417
  14.1 1.6 %collective-permute-start.4 = (bf16[2,128,512]{2,1,0:T(8,128)(2,1)S(1)}, bf16[2,128,512]{2,1,0:T(8,128)(2,1)S(1)}, u32[]{:S(2)}, u32[]{:S(2)}) collective-permute-start(bf16[2,128,512]{2,1,0:T(8,128)(2,1)S(1)} %pad_maximum_fusion), channel_id=1, source_target_pairs={{0,1},{1,0},{2,3},{3,2},{4,5},{5,4},{6,7},{7,6},{8,9},{9,8},{10,11... | collective-permute-start | bytes 786440 | tf_op jit(solution)/shard_map/ppermute | solution.py:388
  15.7 0.8 %copy-start = (bf16[2,256,512]{2,1,0:T(8,128)(2,1)}, bf16[2,256,512]{2,1,0:T(8,128)(2,1)S(1)}, u32[]{:S(2)}) copy-start(bf16[2,256,512]{2,1,0:T(8,128)(2,1)S(1)} %constant_dynamic-update-slice_fusion.text_in) | copy-start | bytes 1572868
  24.7 35.8 %collective-permute-start.8 = (bf16[1024,512]{1,0:T(8,128)(2,1)}, bf16[1024,512]{1,0:T(8,128)(2,1)}, u32[]{:S(2)}, u32[]{:S(2)}) collective-permute-start(bf16[1024,512]{1,0:T(8,128)(2,1)} %v_in.1), channel_id=1, source_target_pairs={{1,2},{3,4},{5,6},{7,8},{9,10},{11,12},{13,14},{2,1},{4,3},{6,5},{... | collective-permute-start | bytes 3145736 | tf_op jit(solution)/shard_map/ppermute | solution.py:451

commit v3 on v2

--- a/solution.py
+++ b/solution.py
@@ -12,7 +12,7 @@
 HEADS = 4
 BLOCK = 128
 REACH = 8
-GROUP = 16
+GROUP = 24
 EXP2_SCALE = HEAD_DIM ** (-0.5) * math.log2(math.e)
 NEVER = -1e30
 NT = (((1,), (1,)), ((), ()))
@@ -336,6 +336,7 @@
     v_outer,
     out_ref,
     v_far,
+    near_rows,
     total_rows,
     weights_all,
     sems,
@@ -348,20 +349,18 @@
         part = pl.ds(pl.multiple_of(group * GROUP, GROUP), GROUP)
         return pltpu.make_async_copy(weights.at[part], weights_all.at[part], weight_sems.at[group])
 
-    copies = [
-        pltpu.make_async_copy(v_outer, v_far, sems.at[0]),
-        pltpu.make_async_copy(near, total_rows, sems.at[1]),
-    ]
-    for copy in copies:
-        copy.start()
+    values_copy = pltpu.make_async_copy(v_outer, v_far, sems.at[0])
+    near_copy = pltpu.make_async_copy(near, near_rows, sems.at[1])
+    values_copy.start()
 
     def begin(group, carry):
         weight_copy(group).start()
         return carry
 
     lax.fori_loop(0, groups, begin, 0)
-    for copy in copies:
-        copy.wait()
+    near_copy.start()
+    total_rows[...] = jnp.zeros(total_rows.shape, jnp.float32)
+    values_copy.wait()
 
     def body(slots):
         weight_copy(slots[0][0] // GROUP).wait()
@@ -378,7 +377,8 @@
             total_rows[aligned(slot[4]), aligned(slot[3])] += part
 
     for_groups(count, far_items, blocks_dev, body)
-    out_ref[...] = total_rows[...].astype(jnp.bfloat16)
+    near_copy.wait()
+    out_ref[...] = (total_rows[...] + near_rows[...]).astype(jnp.bfloat16)
 
 
 def text_step(text, distances):
@@ -517,6 +517,7 @@
         scratch_shapes=[
             pltpu.VMEM((tokens, columns), jnp.bfloat16),
             pltpu.VMEM((tokens, columns), jnp.float32),
+            pltpu.VMEM((tokens, columns), jnp.float32),
             pltpu.VMEM(weights_shape, jnp.bfloat16),
             pltpu.SemaphoreType.DMA((2,)),
             pltpu.SemaphoreType.DMA((room // GROUP,)),

time: 66.6 us -> 66.4 us (level)
  the two profiles are of different devices: /device:TPU:9 before, /device:TPU:1 now
where the time goes in v3:
time: 66.4 us; the launch traced here: 65.9 us
  Pallas kernels  39.8 us (60%)
  starting transfers between devices  18.7 us (28%)
  waiting for transfers between devices  4.97 us (7%)
  other arithmetic  1.5 us (2%)
  local copies, waits for them, and re-layouts  0.83 us (1%)
    pallas_call x1, Pallas kernels, on_device(): pl.pallas_call(functools.partial(near_kernel, blocks_dev), out_shape=(jax...  16.6 us
    pallas_call x1, Pallas kernels, on_device(): pl.pallas_call(functools.partial(text_kernel, blocks_dev), out_shape=(jax...  8.92 us
    pallas_call x1, Pallas kernels, on_device(): pl.pallas_call(functools.partial(middle_kernel, blocks_dev), out_shape=(j...  8.9 us
    ppermute x5, starting transfers between devices, text_step(): lax.ppermute(text, 'seq', [(i, i ^ distance) for i in range(count)])  8.36 us
    ppermute x1, starting transfers between devices, on_device(): k_outer = lax.ppermute(keys, 'seq', outer)  6 us
    pallas_call x1, Pallas kernels, on_device(): pl.pallas_call(functools.partial(last_kernel, blocks_dev), out_shape=jax....  5.45 us
    ppermute x1, starting transfers between devices, on_device(): v_outer = lax.ppermute(values, 'seq', outer)  3.33 us
    ppermute x1, waiting for transfers between devices, on_device(): v_outer = lax.ppermute(values, 'seq', outer)  2.33 us
  transfers between devices with their start and end apart: 9, of which 4 were waited for; matrix products, arithmetic and copies ran while one was open for 1% of the time, Pallas kernels for 52%

profile of v3, /device:TPU:1, one launch (start us, length us, event | category | flops | bytes accessed | tf_op | source)
XLA Modules:
  0.0 65.9 jit_solution(13818516207880435485)
XLA Ops:
  0.0 0.7 %pad_maximum_fusion.2 = bf16[2,16,512]{2,1,0:T(8,128)(2,1)S(1)} fusion(bf16[1,16,512]{2,1,0:T(8,128)(2,1)} %bitcast.2, bf16[1,16,512]{2,1,0:T(8,128)(2,1)} %bitcast.4), kind=kLoop, calls=%fused_computation.2 | loop fusion | flops 16384 | bytes 65536 | tf_op jit(solution)/shard_map/stack | solution.py:415
  0.7 2.0 %collective-permute-start = (bf16[2,16,512]{2,1,0:T(8,128)(2,1)S(1)}, bf16[2,16,512]{2,1,0:T(8,128)(2,1)S(1)}, u32[]{:S(2)}, u32[]{:S(2)}) collective-permute-start(bf16[2,16,512]{2,1,0:T(8,128)(2,1)S(1)} %pad_maximum_fusion.2), channel_id=1, source_target_pairs={{0,2},{1,3},{2,0},{3,1},{4,6},{5,7},{6,4},{7,5},{8,10},{9,11},{10,... | collective-permute-start | bytes 98312 | tf_op jit(solution)/shard_map/ppermute | solution.py:388
  2.8 1.0 %collective-permute-start.6 = (bf16[1024,512]{1,0:T(8,128)(2,1)}, bf16[1024,512]{1,0:T(8,128)(2,1)}, u32[]{:S(2)}, u32[]{:S(2)}) collective-permute-start(bf16[1024,512]{1,0:T(8,128)(2,1)} %k_in.1), channel_id=1, source_target_pairs={{0,1},{1,0},{2,3},{3,2},{4,5},{5,4},{6,7},{7,6},{8,9},{9,8},{10,11... | collective-permute-start | bytes 3145736 | tf_op jit(solution)/shard_map/ppermute | solution.py:418
  3.7 0.0 collective-permute-start.7
  3.7 0.3 collective-permute-done
  4.1 0.7 %pad_maximum_fusion.1 = bf16[2,32,512]{2,1,0:T(8,128)(2,1)S(1)} fusion(bf16[2,16,512]{2,1,0:T(8,128)(2,1)S(1)} %collective-permute-done, bf16[1,16,512]{2,1,0:T(8,128)(2,1)} %bitcast.3, bf16[1,16,512]{2,1,0:T(8,128)(2,1)} %bitcast.5), kind=kLoop, calls=%fused_computation.1 | loop fusion | flops 196608 | bytes 131072 | tf_op jit(solution)/shard_map/concatenate | solution.py:389
  4.8 1.5 %collective-permute-start.1 = (bf16[2,32,512]{2,1,0:T(8,128)(2,1)S(1)}, bf16[2,32,512]{2,1,0:T(8,128)(2,1)S(1)}, u32[]{:S(2)}, u32[]{:S(2)}) collective-permute-start(bf16[2,32,512]{2,1,0:T(8,128)(2,1)S(1)} %pad_maximum_fusion.1), channel_id=1, source_target_pairs={{0,4},{1,5},{2,6},{3,7},{4,0},{5,1},{6,2},{7,3},{8,12},{9,13},{10,... | collective-permute-start | bytes 196616 | tf_op jit(solution)/shard_map/ppermute | solution.py:388
  6.4 2.3 %collective-permute-start.2 = (bf16[2,32,512]{2,1,0:T(8,128)(2,1)S(1)}, bf16[2,32,512]{2,1,0:T(8,128)(2,1)S(1)}, u32[]{:S(2)}, u32[]{:S(2)}) collective-permute-start(bf16[2,32,512]{2,1,0:T(8,128)(2,1)S(1)} %pad_maximum_fusion.1), channel_id=1, source_target_pairs={{0,8},{1,9},{2,10},{3,11},{4,12},{5,13},{6,14},{7,15},{8,0},{9,1},... | collective-permute-start | bytes 196616 | tf_op jit(solution)/shard_map/ppermute | solution.py:388
  8.7 0.0 collective-permute-start.3
  8.7 0.0 collective-permute-done.1
  8.7 6.0 %collective-permute-start.5 = (bf16[1024,512]{1,0:T(8,128)(2,1)}, bf16[1024,512]{1,0:T(8,128)(2,1)}, u32[]{:S(2)}, u32[]{:S(2)}) collective-permute-start(bf16[1024,512]{1,0:T(8,128)(2,1)} %k_in.1), channel_id=1, source_target_pairs={{1,2},{3,4},{5,6},{7,8},{9,10},{11,12},{13,14},{2,1},{4,3},{6,5},{... | collective-permute-start | bytes 3145736 | tf_op jit(solution)/shard_map/ppermute | solution.py:417
  14.7 0.0 collective-permute-done.2
  14.7 0.0 collective-permute-done.3
  14.8 2.5 %collective-permute-start.4 = (bf16[2,128,512]{2,1,0:T(8,128)(2,1)S(1)}, bf16[2,128,512]{2,1,0:T(8,128)(2,1)S(1)}, u32[]{:S(2)}, u32[]{:S(2)}) collective-permute-start(bf16[2,128,512]{2,1,0:T(8,128)(2,1)S(1)} %pad_maximum_fusion), channel_id=1, source_target_pairs={{0,1},{1,0},{2,3},{3,2},{4,5},{5,4},{6,7},{7,6},{8,9},{9,8},{10,11... | collective-permute-start | bytes 786440 | tf_op jit(solution)/shard_map/ppermute | solution.py:388
  17.3 1.1 %collective-permute-done.4 = bf16[2,128,512]{2,1,0:T(8,128)(2,1)S(1)} collective-permute-done((bf16[2,128,512]{2,1,0:T(8,128)(2,1)S(1)}, bf16[2,128,512]{2,1,0:T(8,128)(2,1)S(1)}, u32[]{:S(2)}, u32[]{:S(2)}) %collective-permute-start.4) | collective-permute-done | bytes 262176 | tf_op jit(solution)/shard_map/ppermute | solution.py:388
  18.4 0.0 copy-start
  18.4 0.8 %copy-done = bf16[2,256,512]{2,1,0:T(8,128)(2,1)} copy-done((bf16[2,256,512]{2,1,0:T(8,128)(2,1)}, bf16[2,256,512]{2,1,0:T(8,128)(2,1)S(1)}, u32[]{:S(2)}) %copy-start) | copy-done | bytes 524312
  19.2 8.9 %text.1 = (s32[288]{0:T(512)}, s32[264]{0:T(512)}, s32[2]{0:T(128)}, f32[32,1,128]{2,1,0:T(1,128)}, f32[32,1,128]{2,1,0:T(1,128)}, /*index=5*/f32[32,128,128]{2,1,0:T(8,128)}) custom-call(s32[4,8,9]{2,1,0:T(8,128)} %lists.1, s32[4,8]{1,0:T(4,128)} %lengths.1, bf16[1024,512]{1,0:T(8,128)(2,1)} %q_ref.1, bf16[2,256,512]{2,1,0:T(8,128)(2,1)} %copy-done), custom_call_target="tpu_custom_call" | custom-call | flops 1000000 | bytes 10000 | tf_op jit(solution)/shard_map/text/pallas_call | solution.py:427
  28.1 3.3 %collective-permute-start.8 = (bf16[1024,512]{1,0:T(8,128)(2,1)}, bf16[1024,512]{1,0:T(8,128)(2,1)}, u32[]{:S(2)}, u32[]{:S(2)}) collective-permute-start(bf16[1024,512]{1,0:T(8,128)(2,1)} %v_in.1), channel_id=1, source_target_pairs={{1,2},{3,4},{5,6},{7,8},{9,10},{11,12},{13,14},{2,1},{4,3},{6,5},{... | collective-permute-start | bytes 3145736 | tf_op jit(solution)/shard_map/ppermute | solution.py:451
  31.5 0.0 collective-permute-done.6.k_inner
  31.5 0.0 collective-permute-done.7.v_inner
  31.5 16.6 %own.1 = (f32[32,1,128]{2,1,0:T(1,128)}, f32[32,1,128]{2,1,0:T(1,128)}, f32[32,128,128]{2,1,0:T(8,128)}) custom-call(s32[288]{0:T(512)} %get-tuple-element.25.near_items, s32[2]{0:T(128)} %get-tuple-element.22.counts, bf16[1024,512]{1,0:T(8,128)(2,1)} %q_ref.1, bf16[1024,512]{1,0:T(8,128)(2,1)} %k_in.1, bf16[1024,512]{1,0:T(8,128)(2,1)} %v_in.1, ...), custom_call_target="tpu_custom_call" | custom-call | flops 1000000 | bytes 10000 | tf_op jit(solution)/shard_map/own/pallas_call | solution.py:453
  48.1 1.2 %collective-permute-done.5.k_far = bf16[1024,512]{1,0:T(8,128)(2,1)} collective-permute-done((bf16[1024,512]{1,0:T(8,128)(2,1)}, bf16[1024,512]{1,0:T(8,128)(2,1)}, u32[]{:S(2)}, u32[]{:S(2)}) %collective-permute-start.5) | collective-permute-done | bytes 1048608 | tf_op jit(solution)/shard_map/ppermute | solution.py:417
  49.2 8.9 %middle.1 = (f32[1024,512]{1,0:T(8,128)}, bf16[264,128,128]{2,1,0:T(8,128)(2,1)}) custom-call(s32[264]{0:T(512)} %get-tuple-element.21.far_items, s32[2]{0:T(128)} %get-tuple-element.22.counts, bf16[1024,512]{1,0:T(8,128)(2,1)} %q_ref.1, bf16[1024,512]{1,0:T(8,128)(2,1)} %collective-permute-done.5.k_far, f32[32,1,128]{2,1,0:T(1,128)} %get-tuple-element.29.near_tops, ...), custom_call_target="tpu_custom_call" | custom-call | flops 1000000 | bytes 10000 | tf_op jit(solution)/shard_map/middle/pallas_call | solution.py:487
  58.1 2.3 %collective-permute-done.8.v_outer = bf16[1024,512]{1,0:T(8,128)(2,1)} collective-permute-done((bf16[1024,512]{1,0:T(8,128)(2,1)}, bf16[1024,512]{1,0:T(8,128)(2,1)}, u32[]{:S(2)}, u32[]{:S(2)}) %collective-permute-start.8) | collective-permute-done | bytes 1048608 | tf_op jit(solution)/shard_map/ppermute | solution.py:451
  60.5 5.5 %last.1 = bf16[1024,512]{1,0:T(8,128)(2,1)} custom-call(s32[264]{0:T(512)} %get-tuple-element.21.far_items, s32[2]{0:T(128)} %get-tuple-element.22.counts, f32[1024,512]{1,0:T(8,128)} %get-tuple-element.32.near, bf16[264,128,128]{2,1,0:T(8,128)(2,1)} %get-tuple-element.33.weights, bf16[1024,512]{1,0:T(8,128)(2,1)} %collective-permute-done.8.v_outer), custom_call_target="tpu_custom_call" | custom-call | flops 1000000000 | bytes 9000000 | tf_op jit(solution)/shard_map/last/pallas_call | solution.py:512
  (6 shorter events, 0.1 us)
Async XLA Ops:
  0.7 3.3 %collective-permute-start = (bf16[2,16,512]{2,1,0:T(8,128)(2,1)S(1)}, bf16[2,16,512]{2,1,0:T(8,128)(2,1)S(1)}, u32[]{:S(2)}, u32[]{:S(2)}) collective-permute-start(bf16[2,16,512]{2,1,0:T(8,128)(2,1)S(1)} %pad_maximum_fusion.2), channel_id=1, source_target_pairs={{0,2},{1,3},{2,0},{3,1},{4,6},{5,7},{6,4},{7,5},{8,10},{9,11},{10,... | collective-permute-start | bytes 98312 | tf_op jit(solution)/shard_map/ppermute | solution.py:388
  2.8 28.7 %collective-permute-start.6 = (bf16[1024,512]{1,0:T(8,128)(2,1)}, bf16[1024,512]{1,0:T(8,128)(2,1)}, u32[]{:S(2)}, u32[]{:S(2)}) collective-permute-start(bf16[1024,512]{1,0:T(8,128)(2,1)} %k_in.1), channel_id=1, source_target_pairs={{0,1},{1,0},{2,3},{3,2},{4,5},{5,4},{6,7},{7,6},{8,9},{9,8},{10,11... | collective-permute-start | bytes 3145736 | tf_op jit(solution)/shard_map/ppermute | solution.py:418
  3.7 27.7 %collective-permute-start.7 = (bf16[1024,512]{1,0:T(8,128)(2,1)}, bf16[1024,512]{1,0:T(8,128)(2,1)}, u32[]{:S(2)}, u32[]{:S(2)}) collective-permute-start(bf16[1024,512]{1,0:T(8,128)(2,1)} %v_in.1), channel_id=1, source_target_pairs={{0,1},{1,0},{2,3},{3,2},{4,5},{5,4},{6,7},{7,6},{8,9},{9,8},{10,11... | collective-permute-start | bytes 3145736 | tf_op jit(solution)/shard_map/ppermute | solution.py:419
  4.8 3.9 %collective-permute-start.1 = (bf16[2,32,512]{2,1,0:T(8,128)(2,1)S(1)}, bf16[2,32,512]{2,1,0:T(8,128)(2,1)S(1)}, u32[]{:S(2)}, u32[]{:S(2)}) collective-permute-start(bf16[2,32,512]{2,1,0:T(8,128)(2,1)S(1)} %pad_maximum_fusion.1), channel_id=1, source_target_pairs={{0,4},{1,5},{2,6},{3,7},{4,0},{5,1},{6,2},{7,3},{8,12},{9,13},{10,... | collective-permute-start | bytes 196616 | tf_op jit(solution)/shard_map/ppermute | solution.py:388
  6.4 8.3 %collective-permute-start.2 = (bf16[2,32,512]{2,1,0:T(8,128)(2,1)S(1)}, bf16[2,32,512]{2,1,0:T(8,128)(2,1)S(1)}, u32[]{:S(2)}, u32[]{:S(2)}) collective-permute-start(bf16[2,32,512]{2,1,0:T(8,128)(2,1)S(1)} %pad_maximum_fusion.1), channel_id=1, source_target_pairs={{0,8},{1,9},{2,10},{3,11},{4,12},{5,13},{6,14},{7,15},{8,0},{9,1},... | collective-permute-start | bytes 196616 | tf_op jit(solution)/shard_map/ppermute | solution.py:388
  8.7 6.0 %collective-permute-start.3 = (bf16[2,32,512]{2,1,0:T(8,128)(2,1)S(1)}, bf16[2,32,512]{2,1,0:T(8,128)(2,1)S(1)}, u32[]{:S(2)}, u32[]{:S(2)}) collective-permute-start(bf16[2,32,512]{2,1,0:T(8,128)(2,1)S(1)} %pad_maximum_fusion.1), channel_id=1, source_target_pairs={{0,12},{1,13},{2,14},{3,15},{4,8},{5,9},{6,10},{7,11},{8,4},{9,5},... | collective-permute-start | bytes 196616 | tf_op jit(solution)/shard_map/ppermute | solution.py:388
  8.7 40.5 %collective-permute-start.5 = (bf16[1024,512]{1,0:T(8,128)(2,1)}, bf16[1024,512]{1,0:T(8,128)(2,1)}, u32[]{:S(2)}, u32[]{:S(2)}) collective-permute-start(bf16[1024,512]{1,0:T(8,128)(2,1)} %k_in.1), channel_id=1, source_target_pairs={{1,2},{3,4},{5,6},{7,8},{9,10},{11,12},{13,14},{2,1},{4,3},{6,5},{... | collective-permute-start | bytes 3145736 | tf_op jit(solution)/shard_map/ppermute | solution.py:417
  14.8 3.6 %collective-permute-start.4 = (bf16[2,128,512]{2,1,0:T(8,128)(2,1)S(1)}, bf16[2,128,512]{2,1,0:T(8,128)(2,1)S(1)}, u32[]{:S(2)}, u32[]{:S(2)}) collective-permute-start(bf16[2,128,512]{2,1,0:T(8,128)(2,1)S(1)} %pad_maximum_fusion), channel_id=1, source_target_pairs={{0,1},{1,0},{2,3},{3,2},{4,5},{5,4},{6,7},{7,6},{8,9},{9,8},{10,11... | collective-permute-start | bytes 786440 | tf_op jit(solution)/shard_map/ppermute | solution.py:388
  18.4 0.8 %copy-start = (bf16[2,256,512]{2,1,0:T(8,128)(2,1)}, bf16[2,256,512]{2,1,0:T(8,128)(2,1)S(1)}, u32[]{:S(2)}) copy-start(bf16[2,256,512]{2,1,0:T(8,128)(2,1)S(1)} %constant_dynamic-update-slice_fusion.text_in) | copy-start | bytes 1572868
  28.1 32.3 %collective-permute-start.8 = (bf16[1024,512]{1,0:T(8,128)(2,1)}, bf16[1024,512]{1,0:T(8,128)(2,1)}, u32[]{:S(2)}, u32[]{:S(2)}) collective-permute-start(bf16[1024,512]{1,0:T(8,128)(2,1)} %v_in.1), channel_id=1, source_target_pairs={{1,2},{3,4},{5,6},{7,8},{9,10},{11,12},{13,14},{2,1},{4,3},{6,5},{... | collective-permute-start | bytes 3145736 | tf_op jit(solution)/shard_map/ppermute | solution.py:451
